TPU v7x, 32 devices: a whole 2x2x4 slice. The times are simulated.
32 devices in a mesh: tm: 16 (over z, y, core), row: 2 (over x).
Axes of the slice: x: 2, y: 2, z: 4, core: 2. Of those that a mesh axis runs over, the one named last changes fastest.
Arguments:
- wavefront: float32 [128, 2, 256, 256], P('tm', None, 'row'), may hold values from -6 to 6
- particle_phase: float32 [128, 4096], P('tm', 'row'), may hold values from -3.140625 to 3.140625
- particle_energy: float32 [128, 4096], P('tm', 'row'), may hold values from -6 to 6
- row_offset: float32 [128, 4096], P('tm', 'row'), may hold values from -0.5 to 0.5
- row_cell: int32 [128, 4096], P('tm', 'row'), may hold values from 0 to 255, as said below
- col_cell: int32 [128, 4096], P('tm', 'row'), may hold values from 0 to 255
Outputs:
- wavefront_out: float32 [128, 2, 256, 256], P('tm', None, 'row')
- phase_out: float32 [128, 4096], P('tm', 'row')
- energy_out: float32 [128, 4096], P('tm', 'row')
Inputs may be any that keep to these rules, and one draw needn't show every extreme that they name: `row_cell`: the particle at position p of a slice lies in rows 128 * (p // 2048) to 128 * (p // 2048) + 127.
All inputs are finite; a program needn't handle non-finite values.
Results may differ from a plain program's by a relative error of at most 0.0003.
Values sent between devices are 32-bit elements; how exact they have to be, the bound alone decides.
A program may use at most 64 MiB of HBM per device.

v0:
```python
import math

import jax
import jax.numpy as jnp
import ml_dtypes
import numpy as np
from jax import lax
from jax.experimental import pallas as pl
from jax.experimental.pallas import tpu as pltpu
from jax.sharding import PartitionSpec as P

PUSH_GAIN = 0.5
PHASE_ADVANCE = 1.0
SOURCE_GAIN = 1.0
LANES = 512
BF16 = jnp.bfloat16
F32 = jnp.float32


def diffraction_matrix(length):
    number = np.arange(length)
    signed = np.where(number < length // 2, number, number - length).astype(np.float64)
    kernel = np.fft.ifft(np.exp(-1j * math.pi / length * signed * signed))
    return kernel[(number[:, None] - number[None, :]) % length]


def two_parts(matrix):
    high = matrix.astype(ml_dtypes.bfloat16)
    low = (matrix - high.astype(np.float64)).astype(ml_dtypes.bfloat16)
    return high, low


def split(value):
    high = value.astype(BF16)
    return high, (value - high.astype(F32)).astype(BF16)


def sine_cosine(angle):
    count = jnp.round(angle * (2.0 / math.pi))
    rest = angle - count * 1.5703125
    rest = rest - count * 4.837512969970703125e-4
    rest = rest - count * 7.54978995489188216e-8
    quadrant = count.astype(jnp.int32)
    square = rest * rest
    sine = rest + rest * square * (
        -1.6666654611e-1 + square * (8.3321608736e-3 + square * -1.9515295891e-4)
    )
    cosine = 1.0 + square * (
        -0.5 + square * (4.166664568298827e-2 + square * (-1.388731625493765e-3 + square * 2.443315711809948e-5))
    )
    swapped = (quadrant & 1) == 1
    sine_out = jnp.where(swapped, cosine, sine)
    cosine_out = jnp.where(swapped, sine, cosine)
    sine_out = jnp.where((quadrant & 2) == 2, -sine_out, sine_out)
    cosine_out = jnp.where(((quadrant + 1) & 2) == 2, -cosine_out, cosine_out)
    return sine_out, cosine_out


def dot(left, right):
    return jnp.dot(left, right, preferred_element_type=F32)


def push(field, row, col, offset, phase, energy, hot, sampled):
    rows, cols = field.shape[1], field.shape[2]
    half_rows = rows // 2
    window = half_rows + 16
    groups = row.shape[0] // 2
    lanes = row.shape[1]
    cells = lax.broadcasted_iota(jnp.int32, (cols, lanes), 0)
    for half in range(2):
        start = 0 if half == 0 else half_rows - 16
        high, low = split(field[:, pl.ds(start, window), :].reshape(2 * window, cols))
        row_ids = lax.broadcasted_iota(jnp.int32, (window, lanes), 0) + start
        for group in range(groups):
            at = half * groups + group
            here = pl.ds(at, 1)
            one_hot = jnp.where(cells == col[here, :], 1.0, 0.0).astype(BF16)
            hot[:, pl.ds(at * lanes, lanes)] = one_hot
            mixed = dot(high, one_hot) + dot(low, one_hot)
            away = row_ids - row[here, :]
            f = offset[here, :]
            weight = jnp.where(away == -1, 0.5 * (0.5 - f) * (0.5 - f), 0.0)
            weight = jnp.where(away == 0, 0.75 - f * f, weight)
            weight = jnp.where(away == 1, 0.5 * (0.5 + f) * (0.5 + f), weight)
            sampled[0, here, :] = jnp.sum(weight * mixed[:window], axis=0, keepdims=True)
            sampled[1, here, :] = jnp.sum(weight * mixed[window:], axis=0, keepdims=True)
    sine, cosine = sine_cosine(phase)
    energy = energy - PUSH_GAIN * (sampled[0] * cosine - sampled[1] * sine)
    return phase + PHASE_ADVANCE * energy, energy


def deposit(field, row, phase, hot, source):
    rows = field.shape[1]
    half_rows = rows // 2
    groups = row.shape[0] // 2
    lanes = row.shape[1]
    sine, cosine = sine_cosine(phase)
    source[0] = SOURCE_GAIN * cosine
    source[1] = -SOURCE_GAIN * sine
    for half in range(2):
        row_ids = lax.broadcasted_iota(jnp.int32, (half_rows, lanes), 0) + half * half_rows
        total = None
        for group in range(groups):
            at = half * groups + group
            here = pl.ds(at, 1)
            match = row_ids == row[here, :]
            parts = []
            for part in range(2):
                high, low = split(jnp.where(match, source[part, here, :], 0.0))
                parts += [high, low]
            term = lax.dot_general(
                jnp.concatenate(parts, 0),
                hot[:, pl.ds(at * lanes, lanes)],
                (((1,), (1,)), ((), ())),
                preferred_element_type=F32,
            )
            total = term if total is None else total + term
        own = pl.ds(half * half_rows, half_rows)
        for part in range(2):
            first = total[2 * part * half_rows : (2 * part + 1) * half_rows]
            second = total[(2 * part + 1) * half_rows : (2 * part + 2) * half_rows]
            field[part, own, :] += first + second


def diffract(field, out, mat):
    rows, cols = field.shape[1], field.shape[2]
    mat_high, mat_low = mat[0], mat[1]
    wide_high = jnp.concatenate([mat_high[:cols], mat_high[cols:]], 1)
    wide_low = jnp.concatenate([mat_low[:cols], mat_low[cols:]], 1)
    high, low = split(field[...].reshape(2 * rows, cols))
    turned = dot(high, wide_high) + dot(high, wide_low) + dot(low, wide_high)
    real = turned[:rows, :cols] - turned[rows:, cols:]
    imag = turned[:rows, cols:] + turned[rows:, :cols]
    high, low = split(jnp.concatenate([real, imag], 1))
    turned = dot(mat_high, high) + dot(mat_high, low) + dot(mat_low, high)
    out[0] = turned[:rows, :cols] - turned[rows:, cols:]
    out[1] = turned[:rows, cols:] + turned[rows:, :cols]


def step_kernel(field, row, col, offset, phase, energy, mat, out, phase_out, energy_out, hot, work, sampled, source):
    @pl.loop(0, field.shape[0])
    def _(slot):
        work[...] = field[slot]
        new_phase, new_energy = push(
            work, row.at[slot], col.at[slot], offset.at[slot], phase[slot], energy[slot], hot, sampled
        )
        phase_out[slot] = new_phase
        energy_out[slot] = new_energy
        deposit(work, row.at[slot], new_phase, hot, source)
        diffract(work, out.at[slot], mat)


def step(field, cells, mat):
    slots, _, rows, cols = field.shape
    particles = cells[0].shape
    vmem = pl.BlockSpec(memory_space=pltpu.VMEM)
    return pl.pallas_call(
        step_kernel,
        out_shape=(
            jax.ShapeDtypeStruct(field.shape, F32),
            jax.ShapeDtypeStruct(particles, F32),
            jax.ShapeDtypeStruct(particles, F32),
        ),
        in_specs=[vmem] * 7,
        out_specs=(vmem,) * 3,
        scratch_shapes=[
            pltpu.VMEM((cols, particles[1] * particles[2]), BF16),
            pltpu.VMEM((2, rows, cols), F32),
            pltpu.VMEM((2,) + particles[1:], F32),
            pltpu.VMEM((2,) + particles[1:], F32),
        ],
        compiler_params=pltpu.CompilerParams(vmem_limit_bytes=48 * 1024 * 1024),
        cost_estimate=pl.CostEstimate(flops=20 * 10**9, bytes_accessed=4 * 2**20, transcendentals=0),
    )(field, *cells, mat)


def body(wavefront, particle_phase, particle_energy, row_offset, row_cell, col_cell):
    blocks, halves = lax.axis_size("tm"), lax.axis_size("row")
    count = blocks * halves
    me = lax.axis_index("tm") * halves + lax.axis_index("row")
    axes = ("tm", "row")
    incoming = lax.ppermute(wavefront[-1:], "tm", [(i, i + 1) for i in range(blocks - 1)])
    field = jnp.concatenate([incoming, wavefront[:-1]], 0)
    field = lax.all_to_all(field, "row", split_axis=0, concat_axis=2, tiled=True)
    rows, cols = field.shape[2], field.shape[3]
    matrix = diffraction_matrix(cols)
    mat = jnp.asarray(np.stack(two_parts(np.concatenate([matrix.real, matrix.imag], 0))))
    whole = jnp.stack([particle_phase, particle_energy, row_offset, row_cell.astype(F32), col_cell.astype(F32)])
    whole = lax.all_to_all(whole, "row", split_axis=1, concat_axis=2, tiled=True)
    whole = whole.reshape(5, whole.shape[1], -1, LANES)

    def cells(data):
        return (data[3].astype(jnp.int32), data[4].astype(jnp.int32), data[2], data[0], data[1])

    field, phase, energy = step(field, cells(whole), mat)
    whole = jnp.concatenate([phase[None], energy[None], whole[2:]], 0)
    ahead = lax.ppermute(whole[:, :1], axes, [(i, (i - 1) % count) for i in range(count)])
    whole = jnp.concatenate([whole[:, 1:], ahead], 1)
    keep = jnp.where(me == count - 1, 0.0, 1.0)
    field = jnp.concatenate([field[:-1], jnp.where(keep == 0.0, 0.0, field[-1:])], 0)
    field, phase, energy = step(field, cells(whole), mat)
    forward = [(i, (i + 1) % count) for i in range(count)]
    field = jnp.concatenate([lax.ppermute(field[-1:], axes, forward), field[:-1]], 0)
    pair = jnp.stack([phase, energy]).reshape(2, phase.shape[0], -1)
    pair = jnp.concatenate([lax.ppermute(pair[:, -1:], axes, forward), pair[:, :-1]], 1)
    field = lax.all_to_all(field, "row", split_axis=2, concat_axis=0, tiled=True)
    pair = lax.all_to_all(pair, "row", split_axis=2, concat_axis=1, tiled=True)
    return field, pair[0], pair[1]


def solution(mesh):
    specs = (P("tm", None, "row", None),) + (P("tm", "row"),) * 5
    return jax.shard_map(body, mesh=mesh, in_specs=specs, out_specs=specs[:3], check_vma=False)
```

profile of v0, /device:TPU:0, one launch (start us, length us, event | category | flops | bytes accessed | tf_op | source)
XLA Modules:
  0.0 173.9 jit_solution(10485274824064230556)
XLA Ops:
  1.6 2.4 %collective-permute-start = (f32[1,2,128,256]{3,2,1,0:T(8,128)S(1)}, f32[1,2,128,256]{3,2,1,0:T(8,128)S(1)}, u32[]{:S(2)}, u32[]{:S(2)}) collective-permute-start(f32[1,2,128,256]{3,2,1,0:T(8,128)S(1)} %slice.79), channel_id=1, source_target_pairs={{0,2},{2,4},{4,6},{6,8},{8,10},{10,12},{12,14},{14,16},{16,18},{18... | collective-permute-start | bytes 786440 | tf_op jit(solution)/shard_map/ppermute | solution.py:182
  9.6 3.6 %all-to-all-start.1 = ((f32[5,8,2048]{2,0,1:T(8,128)}), f32[5,8,2048]{2,0,1:T(8,128)S(1)}, u32[]{:S(2)}, u32[]{:S(2)}) async-start(f32[5,8,2048]{2,0,1:T(8,128)} %stack.32), calls=%async_computation.1 | async-start | bytes 1048576 | tf_op jit(solution)/shard_map/all_to_all | solution.py:189
  13.2 1.5 slice-done
  14.7 1.5 pad_maximum_fusion.1
  16.2 5.2 %all-to-all-done.1 = f32[5,8,2048]{2,0,1:T(8,128)S(1)} async-done(((f32[5,8,2048]{2,0,1:T(8,128)}), f32[5,8,2048]{2,0,1:T(8,128)S(1)}, u32[]{:S(2)}, u32[]{:S(2)}) %all-to-all-start.1) | async-done | bytes 327712 | tf_op jit(solution)/shard_map/all_to_all | solution.py:189
  21.4 3.8 %all-to-all-start = ((f32[8,2,128,256]{3,2,1,0:T(8,128)}), f32[8,2,128,256]{3,2,1,0:T(8,128)S(1)}, u32[]{:S(2)}, u32[]{:S(2)}) async-start(f32[8,2,128,256]{3,2,1,0:T(8,128)} %pad_maximum_fusion.1), calls=%async_computation | async-start | bytes 4194304 | tf_op jit(solution)/shard_map/all_to_all | solution.py:184
  26.0 25.1 %all-to-all-done = f32[8,2,128,256]{3,2,1,0:T(8,128)S(1)} async-done(((f32[8,2,128,256]{3,2,1,0:T(8,128)}), f32[8,2,128,256]{3,2,1,0:T(8,128)S(1)}, u32[]{:S(2)}, u32[]{:S(2)}) %all-to-all-start) | async-done | bytes 2097184 | tf_op jit(solution)/shard_map/all_to_all | solution.py:184
  52.2 20.0 %shard_map.94 = (f32[4,2,256,256]{3,2,1,0:T(8,128)S(1)}, f32[4,8,512]{2,1,0:T(8,128)S(1)}, f32[4,8,512]{2,1,0:T(8,128)S(1)}) custom-call(f32[4,2,256,256]{3,2,1,0:T(8,128)S(1)} %bitcast.31, s32[4,8,512]{2,1,0:T(8,128)S(1)} %convert_element_type.29.row, s32[4,8,512]{2,1,0:T(8,128)S(1)} %convert_element_type.31.col, f32[4,8,512]{2,1,0:T(8,128)S(1)} %squeeze.28.offset, ...), custom_call_target="tpu_custom_call" | custom-call | flops 20000000000 | bytes 4194304 | tf_op jit(solution)/shard_map/pallas_call | solution.py:157
  72.7 4.2 %collective-permute-done.1 = f32[5,1,8,512]{3,2,1,0:T(8,128)S(1)} collective-permute-done((f32[5,1,8,512]{3,2,1,0:T(8,128)S(1)}, f32[5,1,8,512]{3,2,1,0:T(8,128)S(1)}, u32[]{:S(2)}, u32[]{:S(2)}) %collective-permute-start.1) | collective-permute-done | bytes 81952 | tf_op jit(solution)/shard_map/ppermute | solution.py:197
  77.0 20.0 %shard_map.95 = (f32[4,2,256,256]{3,2,1,0:T(8,128)S(1)}, f32[4,8,512]{2,1,0:T(8,128)S(1)}, f32[4,8,512]{2,1,0:T(8,128)S(1)}) custom-call(f32[4,2,256,256]{3,2,1,0:T(8,128)S(1)} %pad_maximum_fusion.2.field, s32[4,8,512]{2,1,0:T(8,128)S(1)} %get-tuple-element.18.row, s32[4,8,512]{2,1,0:T(8,128)S(1)} %get-tuple-element.19.col, ...), custom_call_target="tpu_custom_call" | custom-call | flops 20000000000 | bytes 4194304 | tf_op jit(solution)/shard_map/pallas_call | solution.py:157
  99.7 4.3 %copy.37 = f32[2,3,4096]{1,0,2:T(2,128)} copy(f32[2,3,4096]{2,1,0:T(4,128)S(1)} %bitcast.43) | data formatting | bytes 196608 | tf_op jit(solution)/shard_map/slice | solution.py:205
  104.0 5.8 %collective-permute-done.3 = f32[2,1,4096]{2,0,1:T(2,128)S(1)} collective-permute-done((f32[2,1,4096]{2,0,1:T(2,128)S(1)}, f32[2,1,4096]{2,0,1:T(2,128)S(1)}, u32[]{:S(2)}, u32[]{:S(2)}) %collective-permute-start.3) | collective-permute-done | bytes 32800 | tf_op jit(solution)/shard_map/ppermute | solution.py:205
  109.8 4.3 %copy.36 = f32[2,1,4096]{1,0,2:T(2,128)} copy(f32[2,1,4096]{2,0,1:T(2,128)S(1)} %collective-permute-done.3) | data formatting | bytes 65536 | tf_op jit(solution)/shard_map/ppermute | solution.py:205
  114.1 8.1 %fusion.13 = f32[4096,2,4]{2,1,0:T(2,128)} fusion(f32[2,3,4096]{1,0,2:T(2,128)} %copy.37, f32[2,1,4096]{1,0,2:T(2,128)} %copy.36), kind=kLoop, calls=%fused_computation.34 | loop fusion | flops 32768 | bytes 262144
  122.2 8.7 %reshape.32 = f32[2,1,16384]{2,1,0:T(1,128)} reshape(f32[4096,2,4]{2,1,0:T(2,128)} %fusion.13) | data formatting | bytes 262144
  130.9 3.4 %all-to-all-start.3 = ((f32[2,1,16384]{2,1,0:T(1,128)}), f32[2,1,16384]{2,1,0:T(1,128)S(1)}, u32[]{:S(2)}, u32[]{:S(2)}) async-start(f32[2,1,16384]{2,1,0:T(1,128)} %reshape.32), calls=%async_computation.3 | async-start | bytes 262144 | tf_op jit(solution)/shard_map/all_to_all | solution.py:207
  134.4 2.9 %copy.33 = f32[4,2,256,256]{3,1,0,2:T(2,128)} copy(f32[4,2,256,256]{3,2,1,0:T(8,128)S(1)} %pad_maximum_fusion.3) | data formatting | bytes 4194304 | tf_op jit(solution)/shard_map/concatenate | solution.py:203
  137.4 2.0 %all-to-all-done.3 = f32[2,1,16384]{2,1,0:T(1,128)S(1)} async-done(((f32[2,1,16384]{2,1,0:T(1,128)}), f32[2,1,16384]{2,1,0:T(1,128)S(1)}, u32[]{:S(2)}, u32[]{:S(2)}) %all-to-all-start.3) | async-done | bytes 131104 | tf_op jit(solution)/shard_map/all_to_all | solution.py:207
  139.4 4.0 %all-to-all-start.2 = ((f32[4,2,256,256]{3,1,0,2:T(2,128)}), f32[4,2,256,256]{3,1,0,2:T(2,128)S(1)}, u32[]{:S(2)}, u32[]{:S(2)}) async-start(f32[4,2,256,256]{3,1,0,2:T(2,128)} %copy.33), calls=%async_computation.2 | async-start | bytes 4194304 | tf_op jit(solution)/shard_map/all_to_all | solution.py:206
  144.9 8.6 %reshape.33 = f32[4096,2,4]{2,1,0:T(2,128)} reshape(f32[2,16384]{1,0:T(2,128)S(1)} %reduce) | data formatting | bytes 262144
  153.6 8.1 %fusion.11 = (f32[1,2,4,2048]{2,0,3,1:T(1,128)}, f32[1,2,4,2048]{2,0,3,1:T(1,128)}) fusion(f32[2,2,4,2048]{2,0,3,1:T(2,128)} %bitcast.36), kind=kLoop, calls=%fused_computation.32 | loop fusion | bytes 262144 | tf_op jit(solution)/shard_map/slice | solution.py:208
  161.7 4.4 %copy.38 = f32[1,2,4,2048]{3,2,1,0:T(4,128)S(1)} copy(f32[1,2,4,2048]{2,0,3,1:T(1,128)} %get-tuple-element.16) | data formatting | bytes 131072 | tf_op jit(solution)/shard_map/slice | solution.py:208
  166.8 4.4 %copy.39 = f32[1,2,4,2048]{3,2,1,0:T(4,128)S(1)} copy(f32[1,2,4,2048]{2,0,3,1:T(1,128)} %get-tuple-element.15) | data formatting | bytes 131072 | tf_op jit(solution)/shard_map/slice | solution.py:208
  171.9 1.9 %copy.34 = f32[2,4,2,128,256]{4,3,2,1,0:T(8,128)} copy(f32[2,4,2,128,256]{4,2,1,3,0:T(2,128)S(1)} %bitcast.38) | data formatting | bytes 4194304 | tf_op jit(solution)/shard_map/all_to_all | solution.py:206
  (50 shorter events, 14.5 us)
Async XLA Ops:
  1.6 11.6 %collective-permute-start = (f32[1,2,128,256]{3,2,1,0:T(8,128)S(1)}, f32[1,2,128,256]{3,2,1,0:T(8,128)S(1)}, u32[]{:S(2)}, u32[]{:S(2)}) collective-permute-start(f32[1,2,128,256]{3,2,1,0:T(8,128)S(1)} %slice.79), channel_id=1, source_target_pairs={{0,2},{2,4},{4,6},{6,8},{8,10},{10,12},{12,14},{14,16},{16,18},{18... | collective-permute-start | bytes 786440 | tf_op jit(solution)/shard_map/ppermute | solution.py:182
  9.6 11.8 %all-to-all-start.1 = ((f32[5,8,2048]{2,0,1:T(8,128)}), f32[5,8,2048]{2,0,1:T(8,128)S(1)}, u32[]{:S(2)}, u32[]{:S(2)}) async-start(f32[5,8,2048]{2,0,1:T(8,128)} %stack.32), calls=%async_computation.1 | async-start | bytes 1048576 | tf_op jit(solution)/shard_map/all_to_all | solution.py:189
  13.2 1.5 slice-start
  21.4 29.8 %all-to-all-start = ((f32[8,2,128,256]{3,2,1,0:T(8,128)}), f32[8,2,128,256]{3,2,1,0:T(8,128)S(1)}, u32[]{:S(2)}, u32[]{:S(2)}) async-start(f32[8,2,128,256]{3,2,1,0:T(8,128)} %pad_maximum_fusion.1), calls=%async_computation | async-start | bytes 4194304 | tf_op jit(solution)/shard_map/all_to_all | solution.py:184
  51.2 1.0 copy-start
  72.4 4.5 %collective-permute-start.1 = (f32[5,1,8,512]{3,2,1,0:T(8,128)S(1)}, f32[5,1,8,512]{3,2,1,0:T(8,128)S(1)}, u32[]{:S(2)}, u32[]{:S(2)}) collective-permute-start(f32[5,1,8,512]{3,2,1,0:T(8,128)S(1)} %pad_maximum_fusion.5), channel_id=1, source_target_pairs={{0,31},{1,0},{2,1},{3,2},{4,3},{5,4},{6,5},{7,6},{8,7},{9,8},{10,9... | collective-permute-start | bytes 245768 | tf_op jit(solution)/shard_map/ppermute | solution.py:197
  97.0 37.2 %collective-permute-start.2 = (f32[1,2,256,256]{3,2,1,0:T(8,128)S(1)}, f32[1,2,256,256]{3,2,1,0:T(8,128)S(1)}, u32[]{:S(2)}, u32[]{:S(2)}) collective-permute-start(f32[1,2,256,256]{3,2,1,0:T(8,128)S(1)} %slice.97), channel_id=1, source_target_pairs={{0,1},{1,2},{2,3},{3,4},{4,5},{5,6},{6,7},{7,8},{8,9},{9,10},{10,1... | collective-permute-start | bytes 1572872 | tf_op jit(solution)/shard_map/ppermute | solution.py:203
  97.3 12.4 %collective-permute-start.3 = (f32[2,1,4096]{2,0,1:T(2,128)S(1)}, f32[2,1,4096]{2,0,1:T(2,128)S(1)}, u32[]{:S(2)}, u32[]{:S(2)}) collective-permute-start(f32[2,1,4096]{2,0,1:T(2,128)S(1)} %copy.40), channel_id=1, source_target_pairs={{0,1},{1,2},{2,3},{3,4},{4,5},{5,6},{6,7},{7,8},{8,9},{9,10},{10,1... | collective-permute-start | bytes 98312 | tf_op jit(solution)/shard_map/ppermute | solution.py:205
  122.2 12.1 %copy-start.1 = (f32[3,2,256,256]{3,2,1,0:T(8,128)S(1)}, f32[3,2,256,256]{3,2,1,0:T(8,128)}, u32[]{:S(2)}) copy-start(f32[3,2,256,256]{3,2,1,0:T(8,128)} %slice.98) | copy-start | bytes 4718596
  130.9 8.5 %all-to-all-start.3 = ((f32[2,1,16384]{2,1,0:T(1,128)}), f32[2,1,16384]{2,1,0:T(1,128)S(1)}, u32[]{:S(2)}, u32[]{:S(2)}) async-start(f32[2,1,16384]{2,1,0:T(1,128)} %reshape.32), calls=%async_computation.3 | async-start | bytes 262144 | tf_op jit(solution)/shard_map/all_to_all | solution.py:207
  139.4 32.5 %all-to-all-start.2 = ((f32[4,2,256,256]{3,1,0,2:T(2,128)}), f32[4,2,256,256]{3,1,0,2:T(2,128)S(1)}, u32[]{:S(2)}, u32[]{:S(2)}) async-start(f32[4,2,256,256]{3,1,0,2:T(2,128)} %copy.33), calls=%async_computation.2 | async-start | bytes 4194304 | tf_op jit(solution)/shard_map/all_to_all | solution.py:206
where the time goes:
time: 175 us; the launch traced here: 174 us
  local copies, waits for them, and re-layouts  59.5 us (34%)
  waiting for transfers between devices  42.4 us (24%)
  Pallas kernels  40.1 us (23%)
  starting transfers between devices  18.3 us (10%)
  other arithmetic  12.7 us (7%)
    pallas_call x2, Pallas kernels, step(): pl.pallas_call(step_kernel, out_shape=(jax.ShapeDtypeStruct(field.shape,...  40.1 us
    all_to_all x1, waiting for transfers between devices, body(): lax.all_to_all(field, 'row', split_axis=0, concat_axis=2, tiled=True)  25.1 us
    unnamed x8, local copies, waits for them, and re-layouts  18.2 us
    slice x3, local copies, waits for them, and re-layouts, body(): return (field, pair[0], pair[1])  17 us
    unnamed x1, other arithmetic  8.08 us
    ppermute x1, waiting for transfers between devices, body(): lax.ppermute(pair[:, -1:], axes, forward)  5.75 us
    all_to_all x1, waiting for transfers between devices, body(): lax.all_to_all(whole, 'row', split_axis=1, concat_axis=2, tiled=True)  5.21 us
    ppermute x1, local copies, waits for them, and re-layouts, body(): lax.ppermute(pair[:, -1:], axes, forward)  4.34 us
  transfers between devices with their start and end apart: 8, of which 5 were waited for; matrix products, arithmetic and copies ran while one was open for 38% of the time, Pallas kernels for 0%

commit v1 on v0

v1 whole, which is shorter than its diff:
```python
import functools
import math

import jax
import jax.numpy as jnp
import ml_dtypes
import numpy as np
from jax import lax
from jax.experimental import pallas as pl
from jax.experimental.pallas import tpu as pltpu
from jax.sharding import PartitionSpec as P

PUSH_GAIN = 0.5
PHASE_ADVANCE = 1.0
SOURCE_GAIN = 1.0
LANES = 512
BF16 = jnp.bfloat16
F32 = jnp.float32


def diffraction_matrix(length):
    number = np.arange(length)
    signed = np.where(number < length // 2, number, number - length).astype(np.float64)
    kernel = np.fft.ifft(np.exp(-1j * math.pi / length * signed * signed))
    return kernel[(number[:, None] - number[None, :]) % length]


def two_parts(matrix):
    high = matrix.astype(ml_dtypes.bfloat16)
    low = (matrix - high.astype(np.float64)).astype(ml_dtypes.bfloat16)
    return high, low


def split(value):
    high = value.astype(BF16)
    return high, (value - high.astype(F32)).astype(BF16)


def sine_cosine(angle):
    count = jnp.round(angle * (2.0 / math.pi))
    rest = angle - count * 1.5703125
    rest = rest - count * 4.837512969970703125e-4
    rest = rest - count * 7.54978995489188216e-8
    quadrant = count.astype(jnp.int32)
    square = rest * rest
    sine = rest + rest * square * (
        -1.6666654611e-1 + square * (8.3321608736e-3 + square * -1.9515295891e-4)
    )
    cosine = 1.0 + square * (
        -0.5 + square * (4.166664568298827e-2 + square * (-1.388731625493765e-3 + square * 2.443315711809948e-5))
    )
    swapped = (quadrant & 1) == 1
    sine_out = jnp.where(swapped, cosine, sine)
    cosine_out = jnp.where(swapped, sine, cosine)
    sine_out = jnp.where((quadrant & 2) == 2, -sine_out, sine_out)
    cosine_out = jnp.where(((quadrant + 1) & 2) == 2, -cosine_out, cosine_out)
    return sine_out, cosine_out


def dot(left, right):
    return jnp.dot(left, right, preferred_element_type=F32)


def push(field, cell, hot, sampled):
    phase, energy, offset, row, col = (cell.at[item] for item in range(5))
    rows, cols = field.shape[1], field.shape[2]
    half_rows = rows // 2
    window = half_rows + 16
    groups = row.shape[0] // 2
    lanes = row.shape[1]
    cells = lax.broadcasted_iota(jnp.int32, (cols, lanes), 0).astype(F32)
    for half in range(2):
        start = 0 if half == 0 else half_rows - 16
        high, low = split(field[:, pl.ds(start, window), :].reshape(2 * window, cols))
        row_ids = (lax.broadcasted_iota(jnp.int32, (window, lanes), 0) + start).astype(F32)
        for group in range(groups):
            at = half * groups + group
            here = pl.ds(at, 1)
            one_hot = jnp.where(cells == col[here, :], 1.0, 0.0).astype(BF16)
            hot[:, pl.ds(at * lanes, lanes)] = one_hot
            mixed = dot(high, one_hot) + dot(low, one_hot)
            away = row_ids - row[here, :]
            f = offset[here, :]
            weight = jnp.where(away == -1, 0.5 * (0.5 - f) * (0.5 - f), 0.0)
            weight = jnp.where(away == 0, 0.75 - f * f, weight)
            weight = jnp.where(away == 1, 0.5 * (0.5 + f) * (0.5 + f), weight)
            sampled[0, here, :] = jnp.sum(weight * mixed[:window], axis=0, keepdims=True)
            sampled[1, here, :] = jnp.sum(weight * mixed[window:], axis=0, keepdims=True)
    sine, cosine = sine_cosine(phase[...])
    energy[...] = energy[...] - PUSH_GAIN * (sampled[0] * cosine - sampled[1] * sine)
    phase[...] = phase[...] + PHASE_ADVANCE * energy[...]


def deposit(field, cell, hot, source):
    phase, row = cell[0], cell.at[3]
    rows = field.shape[1]
    half_rows = rows // 2
    groups = row.shape[0] // 2
    lanes = row.shape[1]
    sine, cosine = sine_cosine(phase)
    source[0] = SOURCE_GAIN * cosine
    source[1] = -SOURCE_GAIN * sine
    for half in range(2):
        row_ids = (lax.broadcasted_iota(jnp.int32, (half_rows, lanes), 0) + half * half_rows).astype(F32)
        total = None
        for group in range(groups):
            at = half * groups + group
            here = pl.ds(at, 1)
            match = row_ids == row[here, :]
            parts = []
            for part in range(2):
                high, low = split(jnp.where(match, source[part, here, :], 0.0))
                parts += [high, low]
            term = lax.dot_general(
                jnp.concatenate(parts, 0),
                hot[:, pl.ds(at * lanes, lanes)],
                (((1,), (1,)), ((), ())),
                preferred_element_type=F32,
            )
            total = term if total is None else total + term
        own = pl.ds(half * half_rows, half_rows)
        for part in range(2):
            first = total[2 * part * half_rows : (2 * part + 1) * half_rows]
            second = total[(2 * part + 1) * half_rows : (2 * part + 2) * half_rows]
            field[part, own, :] += first + second


def diffract(field, out, mat):
    rows, cols = field.shape[1], field.shape[2]
    mat_high, mat_low = mat[0], mat[1]
    wide_high = jnp.concatenate([mat_high[:cols], mat_high[cols:]], 1)
    wide_low = jnp.concatenate([mat_low[:cols], mat_low[cols:]], 1)
    high, low = split(field[...].reshape(2 * rows, cols))
    turned = dot(high, wide_high) + dot(high, wide_low) + dot(low, wide_high)
    real = turned[:rows, :cols] - turned[rows:, cols:]
    imag = turned[:rows, cols:] + turned[rows:, :cols]
    high, low = split(jnp.concatenate([real, imag], 1))
    turned = dot(mat_high, high) + dot(mat_high, low) + dot(mat_low, high)
    out[0] = turned[:rows, :cols] - turned[rows:, cols:]
    out[1] = turned[:rows, cols:] + turned[rows:, :cols]


def kernel(
    blocks, wave, phase_in, energy_in, offset_in, row_in, col_in, mat,
    wave_out, phase_out, energy_out,
    field, cells, pack, packed, leave, arrive, hot, sampled, source,
    near_sem, far_send, far_recv, part_send, part_recv, own_sem, hand_sem,
    out_send, out_recv, out_own, out_last, leave_send, leave_recv, leave_last,
):
    t, r = lax.axis_index("tm"), lax.axis_index("row")
    other = 1 - r
    after, before = lax.rem(t + 1, blocks), lax.rem(t + blocks - 1, blocks)
    slots = field.shape[0]
    half_rows = field.shape[2] // 2
    groups = cells.shape[2] // 2
    lanes = cells.shape[3]
    mine, theirs = pl.ds(r * half_rows, half_rows), pl.ds(other * half_rows, half_rows)
    inputs = (phase_in, energy_in, offset_in, row_in, col_in)

    def remote(src, dst, send, recv, where):
        return pltpu.make_async_remote_copy(
            src_ref=src, dst_ref=dst, send_sem=send, recv_sem=recv,
            device_id=where, device_id_type=pl.DeviceIdType.MESH,
        )

    def send_half(slot):
        item = slots * other + slot - 1
        return remote(wave.at[item], field.at[slot, :, mine, :], near_sem.at[0, slot], near_sem.at[1, slot], (t, other))

    def receive_half(slot):
        return remote(wave.at[0], field.at[slot, :, theirs, :], near_sem.at[0, slot], near_sem.at[1, slot], (t, other))

    def send_last(half):
        return remote(
            wave.at[wave.shape[0] - 1], field.at[0, :, pl.ds(half * half_rows, half_rows), :],
            far_send.at[0], far_recv.at[half], (after, 0),
        )

    def own_half(slot):
        return pltpu.make_async_copy(wave.at[slots * r + slot - 1], field.at[slot, :, mine, :], own_sem.at[slot])

    def send_part(slot):
        return remote(pack.at[slot], packed.at[slot], part_send.at[slot], part_recv.at[slot], (t, other))

    def hand_over():
        return remote(
            cells.at[0], cells.at[slots], hand_sem.at[0], hand_sem.at[1], (jnp.where(r == 1, t, before), other)
        )

    def is_last(slot):
        return (r == 1) & (slot == slots - 1)

    def goal(slot):
        last = is_last(slot)
        return jnp.where(last, after, t), jnp.where(last, 0, slots * r + slot + 1)

    def send_out(slot):
        block, item = goal(slot)
        return remote(
            field.at[slot, :, theirs, :], wave_out.at[item], out_send.at[slot], out_recv.at[item], (block, other)
        )

    def send_out_last():
        return remote(field.at[slots - 1, :, mine, :], wave_out.at[0], out_last.at[0], out_recv.at[0], (after, 1))

    def own_out(slot):
        return pltpu.make_async_copy(
            field.at[slot, :, mine, :], wave_out.at[slots * r + slot + 1], out_own.at[slot]
        )

    def send_leave(slot):
        block, item = goal(slot)
        return remote(
            leave.at[slot, other], arrive.at[item], leave_send.at[slot], leave_recv.at[item], (block, other)
        )

    def send_leave_last():
        return remote(leave.at[slots - 1, 1], arrive.at[0], leave_last.at[0], leave_recv.at[0], (after, 1))

    barrier = pltpu.get_barrier_semaphore()
    for peer in ((t, other), (after, 0), (after, 1), (before, 0), (before, 1)):
        pl.semaphore_signal(barrier, inc=1, device_id=peer, device_id_type=pl.DeviceIdType.MESH)

    @pl.loop(0, slots)
    def _(slot):
        for number, ref in enumerate(inputs):
            kept = ref[pl.ds(slots * r + slot, 1), :].astype(F32)
            sent = ref[pl.ds(slots * other + slot, 1), :].astype(F32)
            for group in range(groups):
                piece = slice(group * lanes, (group + 1) * lanes)
                cells[slot, number, pl.ds(r * groups + group, 1), :] = kept[:, piece]
                pack[slot, pl.ds(number * groups + group, 1), :] = sent[:, piece]

    pl.semaphore_wait(barrier, 5)

    @pl.when(t < blocks - 1)
    def _():
        send_last(r).start()

    for slot in range(slots):
        send_part(slot).start()
        if slot == 0:
            @pl.when(r == 0)
            def _():
                send_half(0).start()

            @pl.when(r == 1)
            def _():
                own_half(0).start()
        else:
            send_half(slot).start()
            own_half(slot).start()

    @pl.when((t == 0) & (r == 0))
    def _():
        field[0] = jnp.zeros(field.shape[1:], F32)

    @pl.loop(0, 2 * slots)
    def _(turn):
        ending = turn == 2 * slots - 1
        second = ((turn > 0) & (turn % 2 == 0)) | ending
        slot = jnp.where(ending, slots - 1, jnp.where(turn % 2 == 0, jnp.maximum(turn // 2 - 1, 0), (turn + 1) // 2))
        cell = slot + second.astype(jnp.int32)

        @pl.when(jnp.logical_not(second))
        def _():
            send_part(slot).wait_recv()
            for number in range(5):
                for group in range(groups):
                    cells[slot, number, pl.ds(other * groups + group, 1), :] = packed[
                        slot, pl.ds(number * groups + group, 1), :
                    ]

            @pl.when((r == 1) | (slot > 0))
            def _():
                own_half(slot).wait()
                receive_half(slot).wait_recv()

            @pl.when((r == 0) & (slot == 0) & (t > 0))
            def _():
                send_last(0).wait_recv()
                send_last(1).wait_recv()

        @pl.when(ending)
        def _():
            hand_over().wait_recv()

            @pl.when((r == 1) & (t == blocks - 1))
            def _():
                field[slots - 1] = jnp.zeros(field.shape[1:], F32)

        here = field.at[slot]
        push(here, cells.at[cell], hot, sampled)

        @pl.when(turn == 0)
        def _():
            hand_over().start()

        @pl.when(second)
        def _():
            for half in range(2):
                for number in range(2):
                    leave[slot, half, pl.ds(number * groups, groups), :] = cells[
                        cell, number, half * groups : (half + 1) * groups, :
                    ]
            send_leave(slot).start()

            @pl.when(is_last(slot))
            def _():
                send_leave_last().start()

            @pl.when(jnp.logical_not(is_last(slot)))
            def _():
                arrive[slots * r + slot + 1] = leave[slot, r]

        deposit(here, cells.at[cell], hot, source)
        diffract(here, here, mat)

        @pl.when(second)
        def _():
            send_out(slot).start()

            @pl.when(is_last(slot))
            def _():
                send_out_last().start()

            @pl.when(jnp.logical_not(is_last(slot)))
            def _():
                own_out(slot).start()

    def receive_leave(item):
        return remote(leave.at[0, 0], arrive.at[item], leave_send.at[0], leave_recv.at[item], (t, other))

    def receive_out(item):
        return remote(field.at[0, :, mine, :], wave_out.at[item], out_send.at[0], out_recv.at[item], (t, other))

    receive_leave(0).wait_recv()

    @pl.loop(0, slots)
    def _(slot):
        item = slots * other + slot + 1

        @pl.when(item < 2 * slots)
        def _():
            receive_leave(item).wait_recv()

    for item in range(2 * slots):
        for group in range(groups):
            piece = pl.ds(group * lanes, lanes)
            phase_out[pl.ds(item, 1), piece] = arrive[item, pl.ds(group, 1), :]
            energy_out[pl.ds(item, 1), piece] = arrive[item, pl.ds(groups + group, 1), :]

    @pl.when(t < blocks - 1)
    def _():
        send_last(r).wait_send()

    hand_over().wait_send()
    for slot in range(slots):
        send_part(slot).wait_send()
        if slot == 0:
            @pl.when(r == 0)
            def _():
                send_half(0).wait_send()
        else:
            send_half(slot).wait_send()
        send_leave(slot).wait_send()
        send_out(slot).wait_send()

        @pl.when(is_last(slot))
        def _():
            send_leave_last().wait_send()
            send_out_last().wait_send()

        @pl.when(jnp.logical_not(is_last(slot)))
        def _():
            own_out(slot).wait()

    receive_out(0).wait_recv()

    @pl.loop(0, slots)
    def _(slot):
        item = slots * other + slot + 1

        @pl.when(item < 2 * slots)
        def _():
            receive_out(item).wait_recv()


def body(wavefront, particle_phase, particle_energy, row_offset, row_cell, col_cell):
    items, _, half_rows, cols = wavefront.shape
    slots, rows = items // 2, 2 * half_rows
    width = particle_phase.shape[1]
    groups = width // LANES
    matrix = diffraction_matrix(cols)
    mat = jnp.asarray(np.stack(two_parts(np.concatenate([matrix.real, matrix.imag], 0))))
    vmem = pl.BlockSpec(memory_space=pltpu.VMEM)
    anywhere = pl.BlockSpec(memory_space=pl.ANY)
    dma = pltpu.SemaphoreType.DMA
    padded = -(-5 * groups // 8) * 8
    return pl.pallas_call(
        functools.partial(kernel, lax.axis_size("tm")),
        out_shape=(
            jax.ShapeDtypeStruct(wavefront.shape, F32),
            jax.ShapeDtypeStruct(particle_phase.shape, F32),
            jax.ShapeDtypeStruct(particle_phase.shape, F32),
        ),
        in_specs=[anywhere] + [vmem] * 6,
        out_specs=(anywhere, vmem, vmem),
        scratch_shapes=[
            pltpu.VMEM((slots, 2, rows, cols), F32),
            pltpu.VMEM((slots + 1, 5, 2 * groups, LANES), F32),
            pltpu.VMEM((slots, padded, LANES), F32),
            pltpu.VMEM((slots, padded, LANES), F32),
            pltpu.VMEM((slots, 2, 2 * groups, LANES), F32),
            pltpu.VMEM((items, 2 * groups, LANES), F32),
            pltpu.VMEM((cols, 2 * width), BF16),
            pltpu.VMEM((2, 2 * groups, LANES), F32),
            pltpu.VMEM((2, 2 * groups, LANES), F32),
            dma((2, slots)), dma((1,)), dma((2,)), dma((slots,)), dma((slots,)), dma((slots,)), dma((2,)),
            dma((slots,)), dma((items,)), dma((slots,)), dma((1,)), dma((slots,)), dma((items,)), dma((1,)),
        ],
        compiler_params=pltpu.CompilerParams(
            collective_id=0, has_side_effects=True, vmem_limit_bytes=48 * 1024 * 1024
        ),
        cost_estimate=pl.CostEstimate(flops=40 * 10**9, bytes_accessed=8 * 2**20, transcendentals=0),
    )(wavefront, particle_phase, particle_energy, row_offset, row_cell, col_cell, mat)


def solution(mesh):
    specs = (P("tm", None, "row", None),) + (P("tm", "row"),) * 5
    return jax.shard_map(body, mesh=mesh, in_specs=specs, out_specs=specs[:3], check_vma=False)
```

time: 175 us -> 73.8 us (0.42)
  the two profiles are of different devices: /device:TPU:0 before, /device:TPU:1 now
where the time goes in v1:
time: 73.8 us; the launch traced here: 73.3 us
  Pallas kernels  63.3 us (86%)
  local copies, waits for them, and re-layouts  9.4 us (13%)
    pallas_call x1, Pallas kernels, body(): pl.pallas_call(functools.partial(kernel, lax.axis_size('tm')), out_shape=...  63.3 us
    unnamed x17, local copies, waits for them, and re-layouts  9.4 us

profile of v1, /device:TPU:1, one launch (start us, length us, event | category | flops | bytes accessed | tf_op | source)
XLA Modules:
  0.0 73.3 jit_solution(14937370835535505847)
XLA Ops:
  0.6 0.0 copy-start
  0.6 1.6 %copy-done = f32[8,2,128,256]{3,2,1,0:T(8,128)S(1)} copy-done((f32[8,2,128,256]{3,2,1,0:T(8,128)S(1)}, f32[8,2,128,256]{3,2,1,0:T(8,128)}, u32[]{:S(2)}) %copy-start) | copy-done | bytes 2097176
  2.2 0.0 copy-start.1
  2.2 0.8 %copy-done.1 = f32[8,2048]{1,0:T(8,128)S(1)} copy-done((f32[8,2048]{1,0:T(8,128)S(1)}, f32[8,2048]{1,0:T(8,128)}, u32[]{:S(2)}) %copy-start.1) | copy-done | bytes 65560
  3.1 0.0 copy-start.2
  3.1 0.8 %copy-done.2 = f32[8,2048]{1,0:T(8,128)S(1)} copy-done((f32[8,2048]{1,0:T(8,128)S(1)}, f32[8,2048]{1,0:T(8,128)}, u32[]{:S(2)}) %copy-start.2) | copy-done | bytes 65560
  3.9 0.0 copy-start.3
  3.9 0.8 %copy-done.3 = f32[8,2048]{1,0:T(8,128)S(1)} copy-done((f32[8,2048]{1,0:T(8,128)S(1)}, f32[8,2048]{1,0:T(8,128)}, u32[]{:S(2)}) %copy-start.3) | copy-done | bytes 65560
  4.7 0.0 copy-start.4
  4.7 0.8 %copy-done.4 = s32[8,2048]{1,0:T(8,128)S(1)} copy-done((s32[8,2048]{1,0:T(8,128)S(1)}, s32[8,2048]{1,0:T(8,128)}, u32[]{:S(2)}) %copy-start.4) | copy-done | bytes 65560
  5.6 0.0 copy-start.5
  5.6 0.8 %copy-done.5 = s32[8,2048]{1,0:T(8,128)S(1)} copy-done((s32[8,2048]{1,0:T(8,128)S(1)}, s32[8,2048]{1,0:T(8,128)}, u32[]{:S(2)}) %copy-start.5) | copy-done | bytes 65560
  6.4 0.0 copy-start.6
  6.4 1.0 %copy-done.6 = bf16[2,512,256]{2,1,0:T(8,128)(2,1)S(1)} copy-done((bf16[2,512,256]{2,1,0:T(8,128)(2,1)S(1)}, bf16[2,512,256]{2,1,0:T(8,128)(2,1)}, u32[]{:S(2)}) %copy-start.6) | copy-done | bytes 524312
  7.5 63.3 %shard_map.94 = (f32[8,2,128,256]{3,2,1,0:T(8,128)S(1)}, f32[8,2048]{1,0:T(8,128)S(1)}, f32[8,2048]{1,0:T(8,128)S(1)}) custom-call(f32[8,2,128,256]{3,2,1,0:T(8,128)S(1)} %copy-done, f32[8,2048]{1,0:T(8,128)S(1)} %copy-done.1, f32[8,2048]{1,0:T(8,128)S(1)} %copy-done.2, f32[8,2048]{1,0:T(8,128)S(1)} %copy-done.3, s32[8,2048]{1,0:T(8,128)S(1)} %copy-done.4, ...), custom_call_target="tpu_custom_call" | custom-call | flops 40000000000 | bytes 8388608 | tf_op jit(solution)/shard_map/pallas_call | solution.py:400
  70.8 1.3 %copy.13 = f32[8,2,128,256]{3,2,1,0:T(8,128)} copy(f32[8,2,128,256]{3,2,1,0:T(8,128)S(1)} %get-tuple-element.6) | data formatting | bytes 4194304
  72.1 0.6 copy.14
  72.7 0.6 copy.15
Async XLA Ops:
  0.6 1.6 %copy-start = (f32[8,2,128,256]{3,2,1,0:T(8,128)S(1)}, f32[8,2,128,256]{3,2,1,0:T(8,128)}, u32[]{:S(2)}) copy-start(f32[8,2,128,256]{3,2,1,0:T(8,128)} %wave.1) | copy-start | bytes 6291460
  2.2 0.8 %copy-start.1 = (f32[8,2048]{1,0:T(8,128)S(1)}, f32[8,2048]{1,0:T(8,128)}, u32[]{:S(2)}) copy-start(f32[8,2048]{1,0:T(8,128)} %phase_in.1) | copy-start | bytes 196612
  3.1 0.8 %copy-start.2 = (f32[8,2048]{1,0:T(8,128)S(1)}, f32[8,2048]{1,0:T(8,128)}, u32[]{:S(2)}) copy-start(f32[8,2048]{1,0:T(8,128)} %energy_in.1) | copy-start | bytes 196612
  3.9 0.8 %copy-start.3 = (f32[8,2048]{1,0:T(8,128)S(1)}, f32[8,2048]{1,0:T(8,128)}, u32[]{:S(2)}) copy-start(f32[8,2048]{1,0:T(8,128)} %offset_in.1) | copy-start | bytes 196612
  4.7 0.8 %copy-start.4 = (s32[8,2048]{1,0:T(8,128)S(1)}, s32[8,2048]{1,0:T(8,128)}, u32[]{:S(2)}) copy-start(s32[8,2048]{1,0:T(8,128)} %row_in.1) | copy-start | bytes 196612
  5.6 0.8 %copy-start.5 = (s32[8,2048]{1,0:T(8,128)S(1)}, s32[8,2048]{1,0:T(8,128)}, u32[]{:S(2)}) copy-start(s32[8,2048]{1,0:T(8,128)} %col_in.1) | copy-start | bytes 196612
  6.4 1.0 %copy-start.6 = (bf16[2,512,256]{2,1,0:T(8,128)(2,1)S(1)}, bf16[2,512,256]{2,1,0:T(8,128)(2,1)}, u32[]{:S(2)}) copy-start(bf16[2,512,256]{2,1,0:T(8,128)(2,1)} %constant.2.clone.mat) | copy-start | bytes 1572868

commit v2 on v1

--- a/solution.py
+++ b/solution.py
@@ -57,6 +57,11 @@
     return sine_out, cosine_out
 
 
+def tiled(row, count):
+    tile = jnp.broadcast_to(row, (16, row.shape[1])).astype(BF16)
+    return jnp.concatenate([tile] * (count // 16), 0)
+
+
 def dot(left, right):
     return jnp.dot(left, right, preferred_element_type=F32)
 
@@ -68,22 +73,23 @@
     window = half_rows + 16
     groups = row.shape[0] // 2
     lanes = row.shape[1]
-    cells = lax.broadcasted_iota(jnp.int32, (cols, lanes), 0).astype(F32)
+    cells = lax.broadcasted_iota(jnp.int32, (cols, lanes), 0).astype(F32).astype(BF16)
+    one, zero = jnp.ones((cols, lanes), BF16), jnp.zeros((cols, lanes), BF16)
     for half in range(2):
         start = 0 if half == 0 else half_rows - 16
-        high, low = split(field[:, pl.ds(start, window), :].reshape(2 * window, cols))
+        parts = jnp.concatenate(split(field[:, pl.ds(start, window), :].reshape(2 * window, cols)), 1)
         row_ids = (lax.broadcasted_iota(jnp.int32, (window, lanes), 0) + start).astype(F32)
         for group in range(groups):
             at = half * groups + group
             here = pl.ds(at, 1)
-            one_hot = jnp.where(cells == col[here, :], 1.0, 0.0).astype(BF16)
+            one_hot = jnp.where(cells == tiled(col[here, :], cols), one, zero)
             hot[:, pl.ds(at * lanes, lanes)] = one_hot
-            mixed = dot(high, one_hot) + dot(low, one_hot)
-            away = row_ids - row[here, :]
+            mixed = dot(parts, jnp.concatenate([one_hot, one_hot], 0))
+            place = row[here, :]
             f = offset[here, :]
-            weight = jnp.where(away == -1, 0.5 * (0.5 - f) * (0.5 - f), 0.0)
-            weight = jnp.where(away == 0, 0.75 - f * f, weight)
-            weight = jnp.where(away == 1, 0.5 * (0.5 + f) * (0.5 + f), weight)
+            weight = jnp.where(row_ids == place - 1.0, 0.5 * (0.5 - f) * (0.5 - f), 0.0)
+            weight = jnp.where(row_ids == place, 0.75 - f * f, weight)
+            weight = jnp.where(row_ids == place + 1.0, 0.5 * (0.5 + f) * (0.5 + f), weight)
             sampled[0, here, :] = jnp.sum(weight * mixed[:window], axis=0, keepdims=True)
             sampled[1, here, :] = jnp.sum(weight * mixed[window:], axis=0, keepdims=True)
     sine, cosine = sine_cosine(phase[...])
@@ -100,24 +106,25 @@
     sine, cosine = sine_cosine(phase)
     source[0] = SOURCE_GAIN * cosine
     source[1] = -SOURCE_GAIN * sine
+    one, zero = jnp.ones((half_rows, lanes), BF16), jnp.zeros((half_rows, lanes), BF16)
     for half in range(2):
-        row_ids = (lax.broadcasted_iota(jnp.int32, (half_rows, lanes), 0) + half * half_rows).astype(F32)
-        total = None
+        row_ids = (lax.broadcasted_iota(jnp.int32, (half_rows, lanes), 0) + half * half_rows).astype(F32).astype(BF16)
+        spread = []
         for group in range(groups):
-            at = half * groups + group
-            here = pl.ds(at, 1)
-            match = row_ids == row[here, :]
+            here = pl.ds(half * groups + group, 1)
+            match = jnp.where(row_ids == tiled(row[here, :], half_rows), one, zero)
             parts = []
             for part in range(2):
-                high, low = split(jnp.where(match, source[part, here, :], 0.0))
-                parts += [high, low]
-            term = lax.dot_general(
-                jnp.concatenate(parts, 0),
-                hot[:, pl.ds(at * lanes, lanes)],
-                (((1,), (1,)), ((), ())),
-                preferred_element_type=F32,
-            )
-            total = term if total is None else total + term
+                value = source[part, here, :]
+                high = value.astype(BF16).astype(F32)
+                parts += [match * tiled(high, half_rows), match * tiled(value - high, half_rows)]
+            spread.append(jnp.concatenate(parts, 0))
+        total = lax.dot_general(
+            jnp.concatenate(spread, 1),
+            hot[:, pl.ds(half * groups * lanes, groups * lanes)],
+            (((1,), (1,)), ((), ())),
+            preferred_element_type=F32,
+        )
         own = pl.ds(half * half_rows, half_rows)
         for part in range(2):
             first = total[2 * part * half_rows : (2 * part + 1) * half_rows]
@@ -130,20 +137,22 @@
     mat_high, mat_low = mat[0], mat[1]
     wide_high = jnp.concatenate([mat_high[:cols], mat_high[cols:]], 1)
     wide_low = jnp.concatenate([mat_low[:cols], mat_low[cols:]], 1)
+    wide = jnp.concatenate([wide_high, wide_high, wide_low], 0)
     high, low = split(field[...].reshape(2 * rows, cols))
-    turned = dot(high, wide_high) + dot(high, wide_low) + dot(low, wide_high)
+    turned = dot(jnp.concatenate([high, low, high], 1), wide)
     real = turned[:rows, :cols] - turned[rows:, cols:]
     imag = turned[:rows, cols:] + turned[rows:, :cols]
     high, low = split(jnp.concatenate([real, imag], 1))
-    turned = dot(mat_high, high) + dot(mat_high, low) + dot(mat_low, high)
+    turned = dot(jnp.concatenate([mat_high, mat_high, mat_low], 1), jnp.concatenate([high, low, high], 0))
     out[0] = turned[:rows, :cols] - turned[rows:, cols:]
     out[1] = turned[:rows, cols:] + turned[rows:, :cols]
 
 
 def kernel(
-    blocks, wave, phase_in, energy_in, offset_in, row_in, col_in, mat,
+    blocks, wave, phase_hbm, energy_hbm, offset_hbm, row_hbm, col_hbm, mat_hbm,
     wave_out, phase_out, energy_out,
     field, cells, pack, packed, leave, arrive, hot, sampled, source,
+    phase_in, energy_in, offset_in, row_in, col_in, mat, load_sem,
     near_sem, far_send, far_recv, part_send, part_recv, own_sem, hand_sem,
     out_send, out_recv, out_own, out_last, leave_send, leave_recv, leave_last,
 ):
@@ -156,6 +165,13 @@
     lanes = cells.shape[3]
     mine, theirs = pl.ds(r * half_rows, half_rows), pl.ds(other * half_rows, half_rows)
     inputs = (phase_in, energy_in, offset_in, row_in, col_in)
+    sources = (phase_hbm, energy_hbm, offset_hbm, row_hbm, col_hbm, mat_hbm)
+    loads = [
+        pltpu.make_async_copy(src, dst, load_sem.at[number])
+        for number, (src, dst) in enumerate(zip(sources, inputs + (mat,)))
+    ]
+    for load in loads:
+        load.start()
 
     def remote(src, dst, send, recv, where):
         return pltpu.make_async_remote_copy(
@@ -220,6 +236,9 @@
     barrier = pltpu.get_barrier_semaphore()
     for peer in ((t, other), (after, 0), (after, 1), (before, 0), (before, 1)):
         pl.semaphore_signal(barrier, inc=1, device_id=peer, device_id_type=pl.DeviceIdType.MESH)
+
+    for load in loads[:-1]:
+        load.wait()
 
     @pl.loop(0, slots)
     def _(slot):
@@ -314,6 +333,11 @@
                 arrive[slots * r + slot + 1] = leave[slot, r]
 
         deposit(here, cells.at[cell], hot, source)
+
+        @pl.when(turn == 0)
+        def _():
+            loads[-1].wait()
+
         diffract(here, here, mat)
 
         @pl.when(second)
@@ -404,7 +428,7 @@
             jax.ShapeDtypeStruct(particle_phase.shape, F32),
             jax.ShapeDtypeStruct(particle_phase.shape, F32),
         ),
-        in_specs=[anywhere] + [vmem] * 6,
+        in_specs=[anywhere] * 7,
         out_specs=(anywhere, vmem, vmem),
         scratch_shapes=[
             pltpu.VMEM((slots, 2, rows, cols), F32),
@@ -416,11 +440,15 @@
             pltpu.VMEM((cols, 2 * width), BF16),
             pltpu.VMEM((2, 2 * groups, LANES), F32),
             pltpu.VMEM((2, 2 * groups, LANES), F32),
+            *[pltpu.VMEM(particle_phase.shape, F32)] * 3,
+            *[pltpu.VMEM(particle_phase.shape, jnp.int32)] * 2,
+            pltpu.VMEM(mat.shape, BF16),
+            dma((6,)),
             dma((2, slots)), dma((1,)), dma((2,)), dma((slots,)), dma((slots,)), dma((slots,)), dma((2,)),
             dma((slots,)), dma((items,)), dma((slots,)), dma((1,)), dma((slots,)), dma((items,)), dma((1,)),
         ],
         compiler_params=pltpu.CompilerParams(
-            collective_id=0, has_side_effects=True, vmem_limit_bytes=48 * 1024 * 1024
+            collective_id=0, has_side_effects=True, vmem_limit_bytes=60 * 1024 * 1024
         ),
         cost_estimate=pl.CostEstimate(flops=40 * 10**9, bytes_accessed=8 * 2**20, transcendentals=0),
     )(wavefront, particle_phase, particle_energy, row_offset, row_cell, col_cell, mat)

time: 73.8 us -> 67.5 us (0.915)
  the two profiles are of different devices: /device:TPU:1 before, /device:TPU:0 now
where the time goes in v2:
time: 67.5 us; the launch traced here: 66.3 us
  Pallas kernels  61.3 us (91%)
  local copies, waits for them, and re-layouts  4.4 us (7%)
    pallas_call x1, Pallas kernels, body(): pl.pallas_call(functools.partial(kernel, lax.axis_size('tm')), out_shape=...  61.3 us
    unnamed x7, local copies, waits for them, and re-layouts  4.4 us

profile of v2, /device:TPU:0, one launch (start us, length us, event | category | flops | bytes accessed | tf_op | source)
XLA Modules:
  0.0 66.3 jit_solution(5271666168813389580)
XLA Ops:
  0.6 61.3 %shard_map.94 = (f32[8,2,128,256]{3,2,1,0:T(8,128)}, f32[8,2048]{1,0:T(8,128)}, f32[8,2048]{1,0:T(8,128)}) custom-call(f32[8,2,128,256]{3,2,1,0:T(8,128)} %wave.1, f32[8,2048]{1,0:T(8,128)} %phase_hbm.1, f32[8,2048]{1,0:T(8,128)} %energy_hbm.1, f32[8,2048]{1,0:T(8,128)} %offset_hbm.1, s32[8,2048]{1,0:T(8,128)} %row_hbm.1, s32[8,2048]{1,0:T(8,128)} %col_hbm.1, ...), custom_call_target="tpu_custom_call" | custom-call | flops 40000000000 | bytes 8388608 | tf_op jit(solution)/shard_map/pallas_call | solution.py:424
  61.9 0.0 copy-start.1
  61.9 0.0 copy-start
  61.9 3.1 %copy.13 = f32[8,2,128,256]{3,2,1,0:T(8,128)} copy(f32[8,2,128,256]{3,2,1,0:T(8,128)} %get-tuple-element.6) | data formatting | bytes 4194304
  65.1 0.0 copy-done.1
  65.1 0.6 copy.14
  65.7 0.0 copy-done
  65.7 0.6 copy.15
Async XLA Ops:
  61.9 3.2 %copy-start.1 = (f32[8,2048]{1,0:T(8,128)S(1)}, f32[8,2048]{1,0:T(8,128)}, u32[]{:S(2)}) copy-start(f32[8,2048]{1,0:T(8,128)} %get-tuple-element.7) | copy-start | bytes 196612
  61.9 3.8 %copy-start = (f32[8,2048]{1,0:T(8,128)S(1)}, f32[8,2048]{1,0:T(8,128)}, u32[]{:S(2)}) copy-start(f32[8,2048]{1,0:T(8,128)} %get-tuple-element.8) | copy-start | bytes 196612

commit v3 on v2

--- a/solution.py
+++ b/solution.py
@@ -195,8 +195,19 @@
     def own_half(slot):
         return pltpu.make_async_copy(wave.at[slots * r + slot - 1], field.at[slot, :, mine, :], own_sem.at[slot])
 
-    def send_part(slot):
-        return remote(pack.at[slot], packed.at[slot], part_send.at[slot], part_recv.at[slot], (t, other))
+    def send_part(pair):
+        return remote(pack.at[pair], packed.at[pair], part_send.at[pair], part_recv.at[pair], (t, other))
+
+    def pack_pair(pair):
+        for slot in range(2 * pair, 2 * pair + 2):
+            for number, ref in enumerate(inputs):
+                kept = ref[pl.ds(slots * r + slot, 1), :].astype(F32)
+                sent = ref[pl.ds(slots * other + slot, 1), :].astype(F32)
+                base = ((slot % 2) * 5 + number) * groups
+                for group in range(groups):
+                    piece = slice(group * lanes, (group + 1) * lanes)
+                    cells[slot, number, pl.ds(r * groups + group, 1), :] = kept[:, piece]
+                    pack[pair, pl.ds(base + group, 1), :] = sent[:, piece]
 
     def hand_over():
         return remote(
@@ -237,38 +248,29 @@
     for peer in ((t, other), (after, 0), (after, 1), (before, 0), (before, 1)):
         pl.semaphore_signal(barrier, inc=1, device_id=peer, device_id_type=pl.DeviceIdType.MESH)
 
-    for load in loads[:-1]:
-        load.wait()
-
-    @pl.loop(0, slots)
-    def _(slot):
-        for number, ref in enumerate(inputs):
-            kept = ref[pl.ds(slots * r + slot, 1), :].astype(F32)
-            sent = ref[pl.ds(slots * other + slot, 1), :].astype(F32)
-            for group in range(groups):
-                piece = slice(group * lanes, (group + 1) * lanes)
-                cells[slot, number, pl.ds(r * groups + group, 1), :] = kept[:, piece]
-                pack[slot, pl.ds(number * groups + group, 1), :] = sent[:, piece]
-
     pl.semaphore_wait(barrier, 5)
 
     @pl.when(t < blocks - 1)
     def _():
         send_last(r).start()
 
-    for slot in range(slots):
-        send_part(slot).start()
-        if slot == 0:
-            @pl.when(r == 0)
-            def _():
-                send_half(0).start()
-
-            @pl.when(r == 1)
-            def _():
-                own_half(0).start()
-        else:
-            send_half(slot).start()
-            own_half(slot).start()
+    @pl.when(r == 0)
+    def _():
+        send_half(0).start()
+
+    @pl.when(r == 1)
+    def _():
+        own_half(0).start()
+
+    for load in loads[:-1]:
+        load.wait()
+    pack_pair(0)
+    send_part(0).start()
+    send_half(1).start()
+    for pair in range(1, slots // 2):
+        pack_pair(pair)
+    for slot in range(1, slots):
+        own_half(slot).start()
 
     @pl.when((t == 0) & (r == 0))
     def _():
@@ -283,11 +285,16 @@
 
         @pl.when(jnp.logical_not(second))
         def _():
-            send_part(slot).wait_recv()
+            pair, base = slot // 2, (slot % 2) * (5 * groups)
+
+            @pl.when(slot % 2 == 0)
+            def _():
+                send_part(pair).wait_recv()
+
             for number in range(5):
                 for group in range(groups):
                     cells[slot, number, pl.ds(other * groups + group, 1), :] = packed[
-                        slot, pl.ds(number * groups + group, 1), :
+                        pair, pl.ds(base + number * groups + group, 1), :
                     ]
 
             @pl.when((r == 1) | (slot > 0))
@@ -299,6 +306,22 @@
             def _():
                 send_last(0).wait_recv()
                 send_last(1).wait_recv()
+
+            @pl.when((slot > 0) | (r == 0))
+            def _():
+                send_half(slot).wait_send()
+
+            @pl.when((slot == 0) & (r == 1) & (t < blocks - 1))
+            def _():
+                send_last(r).wait_send()
+
+            @pl.when(slot < slots - 2)
+            def _():
+                @pl.when(slot % 2 == 0)
+                def _():
+                    send_part(pair + 1).start()
+
+                send_half(slot + 2).start()
 
         @pl.when(ending)
         def _():
@@ -374,19 +397,14 @@
             phase_out[pl.ds(item, 1), piece] = arrive[item, pl.ds(group, 1), :]
             energy_out[pl.ds(item, 1), piece] = arrive[item, pl.ds(groups + group, 1), :]
 
-    @pl.when(t < blocks - 1)
+    @pl.when((r == 0) & (t < blocks - 1))
     def _():
         send_last(r).wait_send()
 
     hand_over().wait_send()
+    for pair in range(slots // 2):
+        send_part(pair).wait_send()
     for slot in range(slots):
-        send_part(slot).wait_send()
-        if slot == 0:
-            @pl.when(r == 0)
-            def _():
-                send_half(0).wait_send()
-        else:
-            send_half(slot).wait_send()
         send_leave(slot).wait_send()
         send_out(slot).wait_send()
 
@@ -420,7 +438,6 @@
     vmem = pl.BlockSpec(memory_space=pltpu.VMEM)
     anywhere = pl.BlockSpec(memory_space=pl.ANY)
     dma = pltpu.SemaphoreType.DMA
-    padded = -(-5 * groups // 8) * 8
     return pl.pallas_call(
         functools.partial(kernel, lax.axis_size("tm")),
         out_shape=(
@@ -428,13 +445,13 @@
             jax.ShapeDtypeStruct(particle_phase.shape, F32),
             jax.ShapeDtypeStruct(particle_phase.shape, F32),
         ),
-        in_specs=[anywhere] * 7,
+        in_specs=[pl.BlockSpec(memory_space=pltpu.HBM)] * 7,
         out_specs=(anywhere, vmem, vmem),
         scratch_shapes=[
             pltpu.VMEM((slots, 2, rows, cols), F32),
             pltpu.VMEM((slots + 1, 5, 2 * groups, LANES), F32),
-            pltpu.VMEM((slots, padded, LANES), F32),
-            pltpu.VMEM((slots, padded, LANES), F32),
+            pltpu.VMEM((slots // 2, 10 * groups, LANES), F32),
+            pltpu.VMEM((slots // 2, 10 * groups, LANES), F32),
             pltpu.VMEM((slots, 2, 2 * groups, LANES), F32),
             pltpu.VMEM((items, 2 * groups, LANES), F32),
             pltpu.VMEM((cols, 2 * width), BF16),
@@ -444,11 +461,11 @@
             *[pltpu.VMEM(particle_phase.shape, jnp.int32)] * 2,
             pltpu.VMEM(mat.shape, BF16),
             dma((6,)),
-            dma((2, slots)), dma((1,)), dma((2,)), dma((slots,)), dma((slots,)), dma((slots,)), dma((2,)),
+            dma((2, slots)), dma((1,)), dma((2,)), dma((slots // 2,)), dma((slots // 2,)), dma((slots,)), dma((2,)),
             dma((slots,)), dma((items,)), dma((slots,)), dma((1,)), dma((slots,)), dma((items,)), dma((1,)),
         ],
         compiler_params=pltpu.CompilerParams(
-            collective_id=0, has_side_effects=True, vmem_limit_bytes=60 * 1024 * 1024
+            collective_id=0, has_side_effects=True, vmem_limit_bytes=48 * 1024 * 1024
         ),
         cost_estimate=pl.CostEstimate(flops=40 * 10**9, bytes_accessed=8 * 2**20, transcendentals=0),
     )(wavefront, particle_phase, particle_energy, row_offset, row_cell, col_cell, mat)

time: 67.5 us -> 72 us (1.067)
  local copies, waits for them, and re-layouts: 4.4 us -> 9.4 us
  Pallas kernels: 61.3 us -> 60.5 us
    unnamed x7 -> x17, local copies, waits for them, and re-layouts: 4.4 us -> 9.4 us
    pallas_call x1, Pallas kernels: 61.3 us -> 60.5 us  [body(): pl.pallas_call(functools.partial(kernel, lax.axis_size('tm')), out_shape=...]
where the time goes in v3:
time: 72 us; the launch traced here: 70.6 us
  Pallas kernels  60.5 us (84%)
  local copies, waits for them, and re-layouts  9.4 us (13%)
    pallas_call x1, Pallas kernels, body(): pl.pallas_call(functools.partial(kernel, lax.axis_size('tm')), out_shape=...  60.5 us
    unnamed x17, local copies, waits for them, and re-layouts  9.4 us

profile of v3, /device:TPU:0, one launch (start us, length us, event | category | flops | bytes accessed | tf_op | source)
XLA Modules:
  0.0 70.6 jit_solution(1731232766726341618)
XLA Ops:
  0.6 0.0 copy-start
  0.6 1.6 %copy-done = f32[8,2,128,256]{3,2,1,0:T(8,128)S(1)} copy-done((f32[8,2,128,256]{3,2,1,0:T(8,128)S(1)}, f32[8,2,128,256]{3,2,1,0:T(8,128)}, u32[]{:S(2)}) %copy-start) | copy-done | bytes 2097176
  2.2 0.0 copy-start.1
  2.2 0.8 %copy-done.1 = f32[8,2048]{1,0:T(8,128)S(1)} copy-done((f32[8,2048]{1,0:T(8,128)S(1)}, f32[8,2048]{1,0:T(8,128)}, u32[]{:S(2)}) %copy-start.1) | copy-done | bytes 65560
  3.1 0.0 copy-start.2
  3.1 0.8 %copy-done.2 = f32[8,2048]{1,0:T(8,128)S(1)} copy-done((f32[8,2048]{1,0:T(8,128)S(1)}, f32[8,2048]{1,0:T(8,128)}, u32[]{:S(2)}) %copy-start.2) | copy-done | bytes 65560
  3.9 0.0 copy-start.3
  3.9 0.8 %copy-done.3 = f32[8,2048]{1,0:T(8,128)S(1)} copy-done((f32[8,2048]{1,0:T(8,128)S(1)}, f32[8,2048]{1,0:T(8,128)}, u32[]{:S(2)}) %copy-start.3) | copy-done | bytes 65560
  4.7 0.0 copy-start.4
  4.7 0.8 %copy-done.4 = s32[8,2048]{1,0:T(8,128)S(1)} copy-done((s32[8,2048]{1,0:T(8,128)S(1)}, s32[8,2048]{1,0:T(8,128)}, u32[]{:S(2)}) %copy-start.4) | copy-done | bytes 65560
  5.6 0.0 copy-start.5
  5.6 0.8 %copy-done.5 = s32[8,2048]{1,0:T(8,128)S(1)} copy-done((s32[8,2048]{1,0:T(8,128)S(1)}, s32[8,2048]{1,0:T(8,128)}, u32[]{:S(2)}) %copy-start.5) | copy-done | bytes 65560
  6.4 0.0 copy-start.6
  6.4 1.0 %copy-done.6 = bf16[2,512,256]{2,1,0:T(8,128)(2,1)S(1)} copy-done((bf16[2,512,256]{2,1,0:T(8,128)(2,1)S(1)}, bf16[2,512,256]{2,1,0:T(8,128)(2,1)}, u32[]{:S(2)}) %copy-start.6) | copy-done | bytes 524312
  7.5 60.5 %shard_map.94 = (f32[8,2,128,256]{3,2,1,0:T(8,128)S(1)}, f32[8,2048]{1,0:T(8,128)S(1)}, f32[8,2048]{1,0:T(8,128)S(1)}) custom-call(f32[8,2,128,256]{3,2,1,0:T(8,128)S(1)} %copy-done, f32[8,2048]{1,0:T(8,128)S(1)} %copy-done.1, f32[8,2048]{1,0:T(8,128)S(1)} %copy-done.2, f32[8,2048]{1,0:T(8,128)S(1)} %copy-done.3, s32[8,2048]{1,0:T(8,128)S(1)} %copy-done.4, ...), custom_call_target="tpu_custom_call" | custom-call | flops 40000000000 | bytes 8388608 | tf_op jit(solution)/shard_map/pallas_call | solution.py:441
  68.0 1.3 %copy.13 = f32[8,2,128,256]{3,2,1,0:T(8,128)} copy(f32[8,2,128,256]{3,2,1,0:T(8,128)S(1)} %get-tuple-element.6) | data formatting | bytes 4194304
  69.3 0.6 copy.14
  70.0 0.6 copy.15
Async XLA Ops:
  0.6 1.6 %copy-start = (f32[8,2,128,256]{3,2,1,0:T(8,128)S(1)}, f32[8,2,128,256]{3,2,1,0:T(8,128)}, u32[]{:S(2)}) copy-start(f32[8,2,128,256]{3,2,1,0:T(8,128)} %wave.1) | copy-start | bytes 6291460
  2.2 0.8 %copy-start.1 = (f32[8,2048]{1,0:T(8,128)S(1)}, f32[8,2048]{1,0:T(8,128)}, u32[]{:S(2)}) copy-start(f32[8,2048]{1,0:T(8,128)} %phase_hbm.1) | copy-start | bytes 196612
  3.1 0.8 %copy-start.2 = (f32[8,2048]{1,0:T(8,128)S(1)}, f32[8,2048]{1,0:T(8,128)}, u32[]{:S(2)}) copy-start(f32[8,2048]{1,0:T(8,128)} %energy_hbm.1) | copy-start | bytes 196612
  3.9 0.8 %copy-start.3 = (f32[8,2048]{1,0:T(8,128)S(1)}, f32[8,2048]{1,0:T(8,128)}, u32[]{:S(2)}) copy-start(f32[8,2048]{1,0:T(8,128)} %offset_hbm.1) | copy-start | bytes 196612
  4.7 0.8 %copy-start.4 = (s32[8,2048]{1,0:T(8,128)S(1)}, s32[8,2048]{1,0:T(8,128)}, u32[]{:S(2)}) copy-start(s32[8,2048]{1,0:T(8,128)} %row_hbm.1) | copy-start | bytes 196612
  5.6 0.8 %copy-start.5 = (s32[8,2048]{1,0:T(8,128)S(1)}, s32[8,2048]{1,0:T(8,128)}, u32[]{:S(2)}) copy-start(s32[8,2048]{1,0:T(8,128)} %col_hbm.1) | copy-start | bytes 196612
  6.4 1.0 %copy-start.6 = (bf16[2,512,256]{2,1,0:T(8,128)(2,1)S(1)}, bf16[2,512,256]{2,1,0:T(8,128)(2,1)}, u32[]{:S(2)}) copy-start(bf16[2,512,256]{2,1,0:T(8,128)(2,1)} %constant.2.clone.mat_hbm) | copy-start | bytes 1572868

commit v4 on v3

--- a/solution.py
+++ b/solution.py
@@ -3,8 +3,6 @@
 
 import jax
 import jax.numpy as jnp
-import ml_dtypes
-import numpy as np
 from jax import lax
 from jax.experimental import pallas as pl
 from jax.experimental.pallas import tpu as pltpu
@@ -16,19 +14,6 @@
 LANES = 512
 BF16 = jnp.bfloat16
 F32 = jnp.float32
-
-
-def diffraction_matrix(length):
-    number = np.arange(length)
-    signed = np.where(number < length // 2, number, number - length).astype(np.float64)
-    kernel = np.fft.ifft(np.exp(-1j * math.pi / length * signed * signed))
-    return kernel[(number[:, None] - number[None, :]) % length]
-
-
-def two_parts(matrix):
-    high = matrix.astype(ml_dtypes.bfloat16)
-    low = (matrix - high.astype(np.float64)).astype(ml_dtypes.bfloat16)
-    return high, low
 
 
 def split(value):
@@ -60,6 +45,16 @@
 def tiled(row, count):
     tile = jnp.broadcast_to(row, (16, row.shape[1])).astype(BF16)
     return jnp.concatenate([tile] * (count // 16), 0)
+
+
+def fill_matrix(mat):
+    length = mat.shape[2]
+    away = lax.broadcasted_iota(jnp.int32, (length, length), 0) - lax.broadcasted_iota(jnp.int32, (length, length), 1)
+    turn = lax.rem(away * away, 2 * length).astype(F32)
+    sine, cosine = sine_cosine((math.pi / length) * turn - math.pi / 4)
+    for number, value in enumerate((cosine, sine)):
+        for part, piece in enumerate(split(value * (1.0 / math.sqrt(length)))):
+            mat[part, pl.ds(number * length, length), :] = piece
 
 
 def dot(left, right):
@@ -149,7 +144,7 @@
 
 
 def kernel(
-    blocks, wave, phase_hbm, energy_hbm, offset_hbm, row_hbm, col_hbm, mat_hbm,
+    blocks, wave, phase_hbm, energy_hbm, offset_hbm, row_hbm, col_hbm,
     wave_out, phase_out, energy_out,
     field, cells, pack, packed, leave, arrive, hot, sampled, source,
     phase_in, energy_in, offset_in, row_in, col_in, mat, load_sem,
@@ -158,6 +153,8 @@
 ):
     t, r = lax.axis_index("tm"), lax.axis_index("row")
     other = 1 - r
+    p = lax.rem(r + t, 2)
+    first_after = lax.rem(t + 1, 2)
     after, before = lax.rem(t + 1, blocks), lax.rem(t + blocks - 1, blocks)
     slots = field.shape[0]
     half_rows = field.shape[2] // 2
@@ -165,10 +162,10 @@
     lanes = cells.shape[3]
     mine, theirs = pl.ds(r * half_rows, half_rows), pl.ds(other * half_rows, half_rows)
     inputs = (phase_in, energy_in, offset_in, row_in, col_in)
-    sources = (phase_hbm, energy_hbm, offset_hbm, row_hbm, col_hbm, mat_hbm)
+    sources = (phase_hbm, energy_hbm, offset_hbm, row_hbm, col_hbm)
     loads = [
         pltpu.make_async_copy(src, dst, load_sem.at[number])
-        for number, (src, dst) in enumerate(zip(sources, inputs + (mat,)))
+        for number, (src, dst) in enumerate(zip(sources, inputs))
     ]
     for load in loads:
         load.start()
@@ -180,7 +177,7 @@
         )
 
     def send_half(slot):
-        item = slots * other + slot - 1
+        item = slots * (1 - p) + slot - 1
         return remote(wave.at[item], field.at[slot, :, mine, :], near_sem.at[0, slot], near_sem.at[1, slot], (t, other))
 
     def receive_half(slot):
@@ -189,11 +186,11 @@
     def send_last(half):
         return remote(
             wave.at[wave.shape[0] - 1], field.at[0, :, pl.ds(half * half_rows, half_rows), :],
-            far_send.at[0], far_recv.at[half], (after, 0),
+            far_send.at[0], far_recv.at[half], (after, first_after),
         )
 
     def own_half(slot):
-        return pltpu.make_async_copy(wave.at[slots * r + slot - 1], field.at[slot, :, mine, :], own_sem.at[slot])
+        return pltpu.make_async_copy(wave.at[slots * p + slot - 1], field.at[slot, :, mine, :], own_sem.at[slot])
 
     def send_part(pair):
         return remote(pack.at[pair], packed.at[pair], part_send.at[pair], part_recv.at[pair], (t, other))
@@ -201,8 +198,8 @@
     def pack_pair(pair):
         for slot in range(2 * pair, 2 * pair + 2):
             for number, ref in enumerate(inputs):
-                kept = ref[pl.ds(slots * r + slot, 1), :].astype(F32)
-                sent = ref[pl.ds(slots * other + slot, 1), :].astype(F32)
+                kept = ref[pl.ds(slots * p + slot, 1), :].astype(F32)
+                sent = ref[pl.ds(slots * (1 - p) + slot, 1), :].astype(F32)
                 base = ((slot % 2) * 5 + number) * groups
                 for group in range(groups):
                     piece = slice(group * lanes, (group + 1) * lanes)
@@ -211,15 +208,16 @@
 
     def hand_over():
         return remote(
-            cells.at[0], cells.at[slots], hand_sem.at[0], hand_sem.at[1], (jnp.where(r == 1, t, before), other)
+            cells.at[0], cells.at[slots], hand_sem.at[0], hand_sem.at[1],
+            (jnp.where(p == 1, t, before), jnp.where(p == 1, other, r)),
         )
 
     def is_last(slot):
-        return (r == 1) & (slot == slots - 1)
+        return (p == 1) & (slot == slots - 1)
 
     def goal(slot):
         last = is_last(slot)
-        return jnp.where(last, after, t), jnp.where(last, 0, slots * r + slot + 1)
+        return jnp.where(last, after, t), jnp.where(last, 0, slots * p + slot + 1)
 
     def send_out(slot):
         block, item = goal(slot)
@@ -228,11 +226,11 @@
         )
 
     def send_out_last():
-        return remote(field.at[slots - 1, :, mine, :], wave_out.at[0], out_last.at[0], out_recv.at[0], (after, 1))
+        return remote(field.at[slots - 1, :, mine, :], wave_out.at[0], out_last.at[0], out_recv.at[0], (after, r))
 
     def own_out(slot):
         return pltpu.make_async_copy(
-            field.at[slot, :, mine, :], wave_out.at[slots * r + slot + 1], out_own.at[slot]
+            field.at[slot, :, mine, :], wave_out.at[slots * p + slot + 1], out_own.at[slot]
         )
 
     def send_leave(slot):
@@ -242,7 +240,7 @@
         )
 
     def send_leave_last():
-        return remote(leave.at[slots - 1, 1], arrive.at[0], leave_last.at[0], leave_recv.at[0], (after, 1))
+        return remote(leave.at[slots - 1, r], arrive.at[0], leave_last.at[0], leave_recv.at[0], (after, r))
 
     barrier = pltpu.get_barrier_semaphore()
     for peer in ((t, other), (after, 0), (after, 1), (before, 0), (before, 1)):
@@ -254,15 +252,15 @@
     def _():
         send_last(r).start()
 
-    @pl.when(r == 0)
+    @pl.when(p == 0)
     def _():
         send_half(0).start()
 
-    @pl.when(r == 1)
+    @pl.when(p == 1)
     def _():
         own_half(0).start()
 
-    for load in loads[:-1]:
+    for load in loads:
         load.wait()
     pack_pair(0)
     send_part(0).start()
@@ -272,7 +270,9 @@
     for slot in range(1, slots):
         own_half(slot).start()
 
-    @pl.when((t == 0) & (r == 0))
+    fill_matrix(mat)
+
+    @pl.when((t == 0) & (p == 0))
     def _():
         field[0] = jnp.zeros(field.shape[1:], F32)
 
@@ -297,21 +297,21 @@
                         pair, pl.ds(base + number * groups + group, 1), :
                     ]
 
-            @pl.when((r == 1) | (slot > 0))
+            @pl.when((p == 1) | (slot > 0))
             def _():
                 own_half(slot).wait()
                 receive_half(slot).wait_recv()
 
-            @pl.when((r == 0) & (slot == 0) & (t > 0))
+            @pl.when((p == 0) & (slot == 0) & (t > 0))
             def _():
                 send_last(0).wait_recv()
                 send_last(1).wait_recv()
 
-            @pl.when((slot > 0) | (r == 0))
+            @pl.when((slot > 0) | (p == 0))
             def _():
                 send_half(slot).wait_send()
 
-            @pl.when((slot == 0) & (r == 1) & (t < blocks - 1))
+            @pl.when((slot == 0) & (p == 1) & (t < blocks - 1))
             def _():
                 send_last(r).wait_send()
 
@@ -327,7 +327,7 @@
         def _():
             hand_over().wait_recv()
 
-            @pl.when((r == 1) & (t == blocks - 1))
+            @pl.when((p == 1) & (t == blocks - 1))
             def _():
                 field[slots - 1] = jnp.zeros(field.shape[1:], F32)
 
@@ -353,13 +353,9 @@
 
             @pl.when(jnp.logical_not(is_last(slot)))
             def _():
-                arrive[slots * r + slot + 1] = leave[slot, r]
+                arrive[slots * p + slot + 1] = leave[slot, r]
 
         deposit(here, cells.at[cell], hot, source)
-
-        @pl.when(turn == 0)
-        def _():
-            loads[-1].wait()
 
         diffract(here, here, mat)
 
@@ -385,7 +381,7 @@
 
     @pl.loop(0, slots)
     def _(slot):
-        item = slots * other + slot + 1
+        item = slots * (1 - p) + slot + 1
 
         @pl.when(item < 2 * slots)
         def _():
@@ -397,7 +393,7 @@
             phase_out[pl.ds(item, 1), piece] = arrive[item, pl.ds(group, 1), :]
             energy_out[pl.ds(item, 1), piece] = arrive[item, pl.ds(groups + group, 1), :]
 
-    @pl.when((r == 0) & (t < blocks - 1))
+    @pl.when((p == 0) & (t < blocks - 1))
     def _():
         send_last(r).wait_send()
 
@@ -421,7 +417,7 @@
 
     @pl.loop(0, slots)
     def _(slot):
-        item = slots * other + slot + 1
+        item = slots * (1 - p) + slot + 1
 
         @pl.when(item < 2 * slots)
         def _():
@@ -433,19 +429,18 @@
     slots, rows = items // 2, 2 * half_rows
     width = particle_phase.shape[1]
     groups = width // LANES
-    matrix = diffraction_matrix(cols)
-    mat = jnp.asarray(np.stack(two_parts(np.concatenate([matrix.real, matrix.imag], 0))))
+    operands = (wavefront, particle_phase, particle_energy, row_offset, row_cell, col_cell)
     vmem = pl.BlockSpec(memory_space=pltpu.VMEM)
     anywhere = pl.BlockSpec(memory_space=pl.ANY)
     dma = pltpu.SemaphoreType.DMA
     return pl.pallas_call(
         functools.partial(kernel, lax.axis_size("tm")),
         out_shape=(
-            jax.ShapeDtypeStruct(wavefront.shape, F32),
-            jax.ShapeDtypeStruct(particle_phase.shape, F32),
-            jax.ShapeDtypeStruct(particle_phase.shape, F32),
+            pltpu.VMEM(wavefront.shape, F32),
+            pltpu.VMEM(particle_phase.shape, F32),
+            pltpu.VMEM(particle_phase.shape, F32),
         ),
-        in_specs=[pl.BlockSpec(memory_space=pltpu.HBM)] * 7,
+        in_specs=[pl.BlockSpec(memory_space=pltpu.HBM)] * 6,
         out_specs=(anywhere, vmem, vmem),
         scratch_shapes=[
             pltpu.VMEM((slots, 2, rows, cols), F32),
@@ -459,8 +454,8 @@
             pltpu.VMEM((2, 2 * groups, LANES), F32),
             *[pltpu.VMEM(particle_phase.shape, F32)] * 3,
             *[pltpu.VMEM(particle_phase.shape, jnp.int32)] * 2,
-            pltpu.VMEM(mat.shape, BF16),
-            dma((6,)),
+            pltpu.VMEM((2, 2 * cols, cols), BF16),
+            dma((5,)),
             dma((2, slots)), dma((1,)), dma((2,)), dma((slots // 2,)), dma((slots // 2,)), dma((slots,)), dma((2,)),
             dma((slots,)), dma((items,)), dma((slots,)), dma((1,)), dma((slots,)), dma((items,)), dma((1,)),
         ],
@@ -468,7 +463,7 @@
             collective_id=0, has_side_effects=True, vmem_limit_bytes=48 * 1024 * 1024
         ),
         cost_estimate=pl.CostEstimate(flops=40 * 10**9, bytes_accessed=8 * 2**20, transcendentals=0),
-    )(wavefront, particle_phase, particle_energy, row_offset, row_cell, col_cell, mat)
+    )(*(pltpu.with_memory_space_constraint(value, pltpu.HBM) for value in operands))
 
 
 def solution(mesh):

time: 72 us -> 66 us (0.917); the launches traced: 70.6 us -> 65.9 us
  local copies, waits for them, and re-layouts: 9.4 us -> 2.58 us
  Pallas kernels: 60.5 us -> 62.7 us
    unnamed x17 -> x3, local copies, waits for them, and re-layouts: 9.4 us -> 2.58 us
    pallas_call x1, Pallas kernels: 60.5 us -> 62.7 us  [body(): pl.pallas_call(functools.partial(kernel, lax.axis_size('tm')), out_shape=...]
where the time goes in v4:
time: 66 us; the launch traced here: 65.9 us
  Pallas kernels  62.7 us (95%)
  local copies, waits for them, and re-layouts  2.58 us (4%)
    pallas_call x1, Pallas kernels, body(): pl.pallas_call(functools.partial(kernel, lax.axis_size('tm')), out_shape=...  62.7 us
    unnamed x3, local copies, waits for them, and re-layouts  2.58 us

profile of v4, /device:TPU:0, one launch (start us, length us, event | category | flops | bytes accessed | tf_op | source)
XLA Modules:
  0.0 65.9 jit_solution(10656273307454358247)
XLA Ops:
  0.6 62.7 %shard_map.85 = (f32[8,2,128,256]{3,2,1,0:T(8,128)S(1)}, f32[8,2048]{1,0:T(8,128)S(1)}, f32[8,2048]{1,0:T(8,128)S(1)}) custom-call(f32[8,2,128,256]{3,2,1,0:T(8,128)} %wave.1, f32[8,2048]{1,0:T(8,128)} %phase_hbm.1, f32[8,2048]{1,0:T(8,128)} %energy_hbm.1, f32[8,2048]{1,0:T(8,128)} %offset_hbm.1, s32[8,2048]{1,0:T(8,128)} %row_hbm.1, s32[8,2048]{1,0:T(8,128)} %col_hbm.1), custom_call_target="tpu_custom_call" | custom-call | flops 40000000000 | bytes 8388608 | tf_op jit(solution)/shard_map/pallas_call | solution.py:436
  63.3 1.3 %copy.12 = f32[8,2,128,256]{3,2,1,0:T(8,128)} copy(f32[8,2,128,256]{3,2,1,0:T(8,128)S(1)} %get-tuple-element.3) | data formatting | bytes 4194304
  64.6 0.6 copy.13
  65.3 0.6 copy.14

commit v5 on v4

--- a/solution.py
+++ b/solution.py
@@ -278,9 +278,11 @@
 
     @pl.loop(0, 2 * slots)
     def _(turn):
-        ending = turn == 2 * slots - 1
-        second = ((turn > 0) & (turn % 2 == 0)) | ending
-        slot = jnp.where(ending, slots - 1, jnp.where(turn % 2 == 0, jnp.maximum(turn // 2 - 1, 0), (turn + 1) // 2))
+        ending = turn == 2 * slots - 2
+        final = turn == 2 * slots - 1
+        second = ((turn > 0) & (turn % 2 == 0)) | final
+        slot = jnp.where(turn % 2 == 0, jnp.maximum(turn // 2 - 1, 0), (turn + 1) // 2)
+        slot = jnp.where(ending, slots - 1, jnp.where(final, slots - 2, slot))
         cell = slot + second.astype(jnp.int32)
 
         @pl.when(jnp.logical_not(second))
@@ -422,6 +424,15 @@
         @pl.when(item < 2 * slots)
         def _():
             receive_out(item).wait_recv()
+
+
+def store_kernel(*refs):
+    sem = refs[-1]
+    copies = [pltpu.make_async_copy(refs[i], refs[3 + i], sem.at[i]) for i in range(3)]
+    for copy in copies:
+        copy.start()
+    for copy in copies:
+        copy.wait()
 
 
 def body(wavefront, particle_phase, particle_energy, row_offset, row_cell, col_cell):
@@ -433,7 +444,7 @@
     vmem = pl.BlockSpec(memory_space=pltpu.VMEM)
     anywhere = pl.BlockSpec(memory_space=pl.ANY)
     dma = pltpu.SemaphoreType.DMA
-    return pl.pallas_call(
+    results = pl.pallas_call(
         functools.partial(kernel, lax.axis_size("tm")),
         out_shape=(
             pltpu.VMEM(wavefront.shape, F32),
@@ -464,6 +475,14 @@
         ),
         cost_estimate=pl.CostEstimate(flops=40 * 10**9, bytes_accessed=8 * 2**20, transcendentals=0),
     )(*(pltpu.with_memory_space_constraint(value, pltpu.HBM) for value in operands))
+    return pl.pallas_call(
+        store_kernel,
+        out_shape=tuple(pltpu.HBM(value.shape, F32) for value in results),
+        in_specs=[anywhere] * 3,
+        out_specs=(anywhere,) * 3,
+        scratch_shapes=[dma((3,))],
+        cost_estimate=pl.CostEstimate(flops=0, bytes_accessed=4 * 2**20, transcendentals=0),
+    )(*(pltpu.with_memory_space_constraint(value, pltpu.VMEM) for value in results))
 
 
 def solution(mesh):

time: 66 us -> 63.5 us (0.962)
  the two profiles are of different devices: /device:TPU:0 before, /device:TPU:6 now
where the time goes in v5:
time: 63.5 us; the launch traced here: 63.4 us
  Pallas kernels  62.7 us (99%)
  between operations  0.64 us (1%)
    pallas_call x1, Pallas kernels, body(): pl.pallas_call(functools.partial(kernel, lax.axis_size('tm')), out_shape=...  61.4 us
    pallas_call x1, Pallas kernels, body(): pl.pallas_call(store_kernel, out_shape=tuple((pltpu.HBM(value.shape, F32)...  1.37 us

profile of v5, /device:TPU:6, one launch (start us, length us, event | category | flops | bytes accessed | tf_op | source)
XLA Modules:
  0.0 63.4 jit_solution(9981654850355063667)
XLA Ops:
  0.6 61.4 %shard_map.85 = (f32[8,2,128,256]{3,2,1,0:T(8,128)S(1)}, f32[8,2048]{1,0:T(8,128)S(1)}, f32[8,2048]{1,0:T(8,128)S(1)}) custom-call(f32[8,2,128,256]{3,2,1,0:T(8,128)} %wave.1, f32[8,2048]{1,0:T(8,128)} %phase_hbm.1, f32[8,2048]{1,0:T(8,128)} %energy_hbm.1, f32[8,2048]{1,0:T(8,128)} %offset_hbm.1, s32[8,2048]{1,0:T(8,128)} %row_hbm.1, s32[8,2048]{1,0:T(8,128)} %col_hbm.1), custom_call_target="tpu_custom_call" | custom-call | flops 40000000000 | bytes 8388608 | tf_op jit(solution)/shard_map/pallas_call | solution.py:447
  62.0 1.4 %shard_map.86 = (f32[8,2,128,256]{3,2,1,0:T(8,128)}, f32[8,2048]{1,0:T(8,128)}, f32[8,2048]{1,0:T(8,128)}) custom-call(f32[8,2,128,256]{3,2,1,0:T(8,128)S(1)} %get-tuple-element.6.refs_0_, f32[8,2048]{1,0:T(8,128)S(1)} %get-tuple-element.7.refs_1_, f32[8,2048]{1,0:T(8,128)S(1)} %get-tuple-element.8.refs_2_), custom_call_target="tpu_custom_call" | custom-call | bytes 4194304 | tf_op jit(solution)/shard_map/pallas_call | solution.py:478

commit v6 on v5

--- a/solution.py
+++ b/solution.py
@@ -267,6 +267,9 @@
     send_half(1).start()
     for pair in range(1, slots // 2):
         pack_pair(pair)
+        send_part(pair).start()
+        send_half(2 * pair).start()
+        send_half(2 * pair + 1).start()
     for slot in range(1, slots):
         own_half(slot).start()
 
@@ -309,21 +312,6 @@
                 send_last(0).wait_recv()
                 send_last(1).wait_recv()
 
-            @pl.when((slot > 0) | (p == 0))
-            def _():
-                send_half(slot).wait_send()
-
-            @pl.when((slot == 0) & (p == 1) & (t < blocks - 1))
-            def _():
-                send_last(r).wait_send()
-
-            @pl.when(slot < slots - 2)
-            def _():
-                @pl.when(slot % 2 == 0)
-                def _():
-                    send_part(pair + 1).start()
-
-                send_half(slot + 2).start()
 
         @pl.when(ending)
         def _():
@@ -395,14 +383,20 @@
             phase_out[pl.ds(item, 1), piece] = arrive[item, pl.ds(group, 1), :]
             energy_out[pl.ds(item, 1), piece] = arrive[item, pl.ds(groups + group, 1), :]
 
-    @pl.when((p == 0) & (t < blocks - 1))
+    @pl.when(t < blocks - 1)
     def _():
         send_last(r).wait_send()
+
+    @pl.when(p == 0)
+    def _():
+        send_half(0).wait_send()
 
     hand_over().wait_send()
     for pair in range(slots // 2):
         send_part(pair).wait_send()
     for slot in range(slots):
+        if slot > 0:
+            send_half(slot).wait_send()
         send_leave(slot).wait_send()
         send_out(slot).wait_send()
 

time: 63.5 us -> 66.9 us (1.054)
  the two profiles are of different devices: /device:TPU:6 before, /device:TPU:0 now
where the time goes in v6:
time: 66.9 us; the launch traced here: 66.8 us
  Pallas kernels  66.1 us (99%)
    pallas_call x1, Pallas kernels, body(): pl.pallas_call(functools.partial(kernel, lax.axis_size('tm')), out_shape=...  64.8 us
    pallas_call x1, Pallas kernels, body(): pl.pallas_call(store_kernel, out_shape=tuple((pltpu.HBM(value.shape, F32)...  1.37 us

profile of v6, /device:TPU:0, one launch (start us, length us, event | category | flops | bytes accessed | tf_op | source)
XLA Modules:
  0.0 66.8 jit_solution(10594253074147778656)
XLA Ops:
  0.6 64.8 %shard_map.85 = (f32[8,2,128,256]{3,2,1,0:T(8,128)S(1)}, f32[8,2048]{1,0:T(8,128)S(1)}, f32[8,2048]{1,0:T(8,128)S(1)}) custom-call(f32[8,2,128,256]{3,2,1,0:T(8,128)} %wave.1, f32[8,2048]{1,0:T(8,128)} %phase_hbm.1, f32[8,2048]{1,0:T(8,128)} %energy_hbm.1, f32[8,2048]{1,0:T(8,128)} %offset_hbm.1, s32[8,2048]{1,0:T(8,128)} %row_hbm.1, s32[8,2048]{1,0:T(8,128)} %col_hbm.1), custom_call_target="tpu_custom_call" | custom-call | flops 40000000000 | bytes 8388608 | tf_op jit(solution)/shard_map/pallas_call | solution.py:441
  65.4 1.4 %shard_map.86 = (f32[8,2,128,256]{3,2,1,0:T(8,128)}, f32[8,2048]{1,0:T(8,128)}, f32[8,2048]{1,0:T(8,128)}) custom-call(f32[8,2,128,256]{3,2,1,0:T(8,128)S(1)} %get-tuple-element.6.refs_0_, f32[8,2048]{1,0:T(8,128)S(1)} %get-tuple-element.7.refs_1_, f32[8,2048]{1,0:T(8,128)S(1)} %get-tuple-element.8.refs_2_), custom_call_target="tpu_custom_call" | custom-call | bytes 4194304 | tf_op jit(solution)/shard_map/pallas_call | solution.py:472

commit v7 on v6

--- a/solution.py
+++ b/solution.py
@@ -264,12 +264,8 @@
         load.wait()
     pack_pair(0)
     send_part(0).start()
-    send_half(1).start()
     for pair in range(1, slots // 2):
         pack_pair(pair)
-        send_part(pair).start()
-        send_half(2 * pair).start()
-        send_half(2 * pair + 1).start()
     for slot in range(1, slots):
         own_half(slot).start()
 
@@ -288,6 +284,18 @@
         slot = jnp.where(ending, slots - 1, jnp.where(final, slots - 2, slot))
         cell = slot + second.astype(jnp.int32)
 
+        @pl.when(turn == 0)
+        def _():
+            @pl.when(p == 0)
+            def _():
+                send_half(0).wait_send()
+
+            @pl.when((p == 1) & (t < blocks - 1))
+            def _():
+                send_last(r).wait_send()
+
+            send_half(1).start()
+
         @pl.when(jnp.logical_not(second))
         def _():
             pair, base = slot // 2, (slot % 2) * (5 * groups)
@@ -320,6 +328,15 @@
             @pl.when((p == 1) & (t == blocks - 1))
             def _():
                 field[slots - 1] = jnp.zeros(field.shape[1:], F32)
+
+        @pl.when(turn == 1)
+        def _():
+            for pair in range(1, slots // 2):
+                send_part(pair).start()
+
+        @pl.when((turn > 0) & (turn < slots - 1))
+        def _():
+            send_half(turn + 1).start()
 
         here = field.at[slot]
         push(here, cells.at[cell], hot, sampled)
@@ -383,13 +400,9 @@
             phase_out[pl.ds(item, 1), piece] = arrive[item, pl.ds(group, 1), :]
             energy_out[pl.ds(item, 1), piece] = arrive[item, pl.ds(groups + group, 1), :]
 
-    @pl.when(t < blocks - 1)
+    @pl.when((p == 0) & (t < blocks - 1))
     def _():
         send_last(r).wait_send()
-
-    @pl.when(p == 0)
-    def _():
-        send_half(0).wait_send()
 
     hand_over().wait_send()
     for pair in range(slots // 2):

time: 66.9 us -> 64.6 us (0.966)
  Pallas kernels: 66.1 us -> 63.8 us
    pallas_call x1, Pallas kernels: 64.8 us -> 62.5 us  [body(): pl.pallas_call(functools.partial(kernel, lax.axis_size('tm')), out_shape=...]
where the time goes in v7:
time: 64.6 us; the launch traced here: 64.5 us
  Pallas kernels  63.8 us (99%)
    pallas_call x1, Pallas kernels, body(): pl.pallas_call(functools.partial(kernel, lax.axis_size('tm')), out_shape=...  62.5 us
    pallas_call x1, Pallas kernels, body(): pl.pallas_call(store_kernel, out_shape=tuple((pltpu.HBM(value.shape, F32)...  1.37 us

profile of v7, /device:TPU:0, one launch (start us, length us, event | category | flops | bytes accessed | tf_op | source)
XLA Modules:
  0.0 64.5 jit_solution(12966221611689992991)
XLA Ops:
  0.6 62.5 %shard_map.85 = (f32[8,2,128,256]{3,2,1,0:T(8,128)S(1)}, f32[8,2048]{1,0:T(8,128)S(1)}, f32[8,2048]{1,0:T(8,128)S(1)}) custom-call(f32[8,2,128,256]{3,2,1,0:T(8,128)} %wave.1, f32[8,2048]{1,0:T(8,128)} %phase_hbm.1, f32[8,2048]{1,0:T(8,128)} %energy_hbm.1, f32[8,2048]{1,0:T(8,128)} %offset_hbm.1, s32[8,2048]{1,0:T(8,128)} %row_hbm.1, s32[8,2048]{1,0:T(8,128)} %col_hbm.1), custom_call_target="tpu_custom_call" | custom-call | flops 40000000000 | bytes 8388608 | tf_op jit(solution)/shard_map/pallas_call | solution.py:454
  63.1 1.4 %shard_map.86 = (f32[8,2,128,256]{3,2,1,0:T(8,128)}, f32[8,2048]{1,0:T(8,128)}, f32[8,2048]{1,0:T(8,128)}) custom-call(f32[8,2,128,256]{3,2,1,0:T(8,128)S(1)} %get-tuple-element.6.refs_0_, f32[8,2048]{1,0:T(8,128)S(1)} %get-tuple-element.7.refs_1_, f32[8,2048]{1,0:T(8,128)S(1)} %get-tuple-element.8.refs_2_), custom_call_target="tpu_custom_call" | custom-call | bytes 4194304 | tf_op jit(solution)/shard_map/pallas_call | solution.py:485
